TPU v7x, 32 devices: a whole 2x2x4 slice. The times are simulated.
32 devices in a mesh: gx: 2 (over y), gy: 4 (over z), gz: 4 (over x, core).
Axes of the slice: x: 2, y: 2, z: 4, core: 2. Of those that a mesh axis runs over, the one named last changes fastest.
Arguments:
- right_side: float32 [8, 8, 2048], P('gx', 'gy', 'gz'), may hold values from -24 to 24
- element_class: int32 [8, 8, 32], P('gx', 'gy', 'gz'), may hold values from 0 to 15
- class_blocks: float32 [16, 64, 64], replicated, may hold values from -0.05 to 11, as said below
- class_shift: float32 [16], replicated, may hold values from 0.5 to 4
- face_weights: float32 [3], replicated, may hold values from 0.4 to 0.9
Outputs:
- solution_field: float32 [8, 8, 2048], P('gx', 'gy', 'gz')
- residual: float32 [8, 8, 2048], P('gx', 'gy', 'gz')
Inputs may be any that keep to these rules, and one draw needn't show every extreme that they name: `class_blocks`: each block is symmetric, and each diagonal entry exceeds the sum of magnitudes of the other entries of its row by 3 or more.
All inputs are finite; a program needn't handle non-finite values.
Results may differ from a plain program's by a relative error of at most 0.00027.
Values sent between devices are 32-bit elements; how exact they have to be, the bound alone decides.
A program may use at most 64 MiB of HBM per device.

v0:
```python
import jax
import jax.numpy as jnp
import numpy as np
from jax import lax
from jax.sharding import PartitionSpec as P

P_SIZE = 64
SWEEPS = 4


highest = lax.Precision.HIGHEST
relax_weight = 0.6


def with_halo(x, sides, width):
    for axis, dim in sides:
        size, length = (lax.axis_size(axis), x.shape[dim])
        up = [(i, (i + 1) % size) for i in range(size - 1)]
        down = [(j, i) for i, j in up]
        last = lax.slice_in_dim(x, length - width, length, axis=dim)
        first = lax.slice_in_dim(x, 0, width, axis=dim)
        before = lax.ppermute(last, axis, up)
        after = lax.ppermute(first, axis, down)
        x = jnp.concatenate([before, x, after], axis=dim)
    return x


def partner_2(x, axis, bit):
    return lax.ppermute(x, axis, [(i, i ^ 1 << bit) for i in range(lax.axis_size(axis))])


def face_tables():
    node_ids = np.arange(P_SIZE)
    digits = (node_ids // 16, node_ids // 4 % 4, node_ids % 4)
    strides = (48, 12, 3)
    lower_sets = [node_ids[digits[axis_dim] == 0] for axis_dim in range(3)]
    return (lower_sets, strides)


def full_matrix(face_weights):
    lower_sets, strides = face_tables()
    pieces = []
    for axis_dim in range(3):
        lower_ids = lower_sets[axis_dim]
        upper_ids = lower_ids + strides[axis_dim]
        from_next = np.zeros((P_SIZE, P_SIZE), np.float32)
        from_next[lower_ids, upper_ids] = 1.0
        from_prev = np.zeros((P_SIZE, P_SIZE), np.float32)
        from_prev[upper_ids, lower_ids] = 1.0
        pieces.append(face_weights[axis_dim] * jnp.asarray(from_next))
        pieces.append(face_weights[axis_dim] * jnp.asarray(from_prev))
    return jnp.concatenate(pieces, axis=0)


def couple_full(cubes, face_weights):
    count = cubes.shape[0] * cubes.shape[1] * cubes.shape[2]
    padded = with_halo(cubes, (("gx", 0), ("gy", 1), ("gz", 2)), 1)
    views = [
        padded[2:, 1:-1, 1:-1],
        padded[:-2, 1:-1, 1:-1],
        padded[1:-1, 2:, 1:-1],
        padded[1:-1, :-2, 1:-1],
        padded[1:-1, 1:-1, 2:],
        padded[1:-1, 1:-1, :-2],
    ]
    stacked = jnp.concatenate(views, axis=3).reshape(count, 6 * P_SIZE)
    return jnp.dot(stacked, full_matrix(face_weights), precision=highest)


def coarsen(values):
    size_x, size_y, size_z = values.shape
    return values.reshape(size_x // 2, 2, size_y // 2, 2, size_z // 2, 2).sum(axis=(1, 3, 5))


def refine(values):
    return jnp.repeat(jnp.repeat(jnp.repeat(values, 2, axis=0), 2, axis=1), 2, axis=2)


def section_apply(values, shift):
    padded = jnp.pad(values, ((1, 1), (1, 1), (1, 1)))
    beside = padded[2:, 1:-1, 1:-1] + padded[:-2, 1:-1, 1:-1]
    beside = beside + padded[1:-1, 2:, 1:-1] + padded[1:-1, :-2, 1:-1]
    beside = beside + padded[1:-1, 1:-1, 2:] + padded[1:-1, 1:-1, :-2]
    return (6.0 + shift) * values - beside


def assemble(stacked, depth, layout):
    undo_list = []
    for axis_dim, axis_count, bit_offset, my_index in layout:
        if axis_count >= 2**depth:
            partner = partner_2(stacked, ("gx", "gy", "gz"), bit_offset + depth - 1)
            upper_half = my_index >> depth - 1 & 1 == 1
            half_size = stacked.shape[axis_dim + 1]
            low_first = jnp.concatenate([stacked, partner], axis_dim + 1)
            high_first = jnp.concatenate([partner, stacked], axis_dim + 1)
            stacked = jnp.where(upper_half, high_first, low_first)
            undo_list.append((axis_dim, upper_half, half_size))
    return (stacked, undo_list)


def unpick(values, undo_list):
    for axis_dim, upper_half, half_size in reversed(undo_list):
        values = lax.dynamic_slice_in_dim(
            values, upper_half.astype(jnp.int32) * half_size, half_size, axis_dim
        )
    return values


def fine_apply(field, operator):
    onehot, wide_blocks, face_weights = operator
    size_x, size_y, width = field.shape
    size_z = width // P_SIZE
    count = size_x * size_y * size_z
    classes = onehot.shape[1]
    flat = field.reshape(count, P_SIZE)
    products = jnp.dot(flat, wide_blocks, precision=highest).reshape(count, classes, P_SIZE)
    local_part = jnp.einsum("ekn,ek->en", products, onehot, precision=highest)
    cubes = field.reshape(size_x, size_y, size_z, P_SIZE)
    nearby = couple_full(cubes, face_weights)
    return (local_part - nearby).reshape(size_x, size_y, width)


def section_cycle(source, shift, depth, layout):
    diagonal = 6.0 + shift
    if depth == 3:
        iterate = jnp.zeros_like(source)
        for sweep_index in range(SWEEPS):
            iterate = iterate + relax_weight * (source - section_apply(iterate, shift)) / diagonal
        return iterate
    iterate = relax_weight * source / diagonal
    remainder = source - section_apply(iterate, shift)
    gathered, undo_list = assemble(
        jnp.stack([0.25 * coarsen(remainder), 0.125 * coarsen(shift)]), depth + 1, layout
    )
    coarse = section_cycle(gathered[0], gathered[1], depth + 1, layout)
    iterate = iterate + refine(unpick(coarse, undo_list))
    return iterate + relax_weight * (source - section_apply(iterate, shift)) / diagonal


def precondition(source, context):
    operator, fine_diagonal, shift_cells, row_totals, layout = context
    iterate = relax_weight * source / fine_diagonal
    remainder = source - fine_apply(iterate, operator)
    size_x, size_y, width = source.shape
    sums = remainder.reshape(size_x, size_y, width // P_SIZE, P_SIZE).sum(axis=3)
    gathered, undo_list = assemble(
        jnp.stack([coarsen(sums) / float(P_SIZE), 0.125 * coarsen(shift_cells)]), 1, layout
    )
    coarse = section_cycle(gathered[0], gathered[1], 1, layout)
    correction = refine(unpick(coarse, undo_list))
    iterate = iterate + jnp.repeat(correction, P_SIZE, axis=2)
    update = source - fine_apply(iterate, operator)
    return iterate + relax_weight * update / fine_diagonal


def total(terms):
    return lax.psum(terms, ("gx", "gy", "gz"))


def per_device(right_side, element_class, class_blocks, class_shift, face_weights):
    size_x, size_y, width = right_side.shape
    size_z = width // P_SIZE
    classes = class_blocks.shape[0]
    element_count = size_x * size_y * size_z
    onehot = (
        element_class.reshape(element_count, 1) == jnp.arange(classes, dtype=jnp.int32)[None, :]
    ).astype(jnp.float32)
    wide_blocks = jnp.transpose(class_blocks, (2, 0, 1)).reshape(P_SIZE, classes * P_SIZE)
    operator = (onehot, wide_blocks, face_weights)
    diag_table = jnp.diagonal(class_blocks, axis1=1, axis2=2)
    fine_diagonal = jnp.dot(onehot, diag_table, precision=highest).reshape(size_x, size_y, width)
    shift_cells = jnp.dot(onehot, class_shift[:, None], precision=highest).reshape(
        size_x, size_y, size_z
    )
    row_totals = None
    bits_z = lax.axis_size("gz").bit_length() - 1
    bits_y = lax.axis_size("gy").bit_length() - 1
    layout = (
        (0, lax.axis_size("gx"), bits_z + bits_y, lax.axis_index("gx")),
        (1, lax.axis_size("gy"), bits_z, lax.axis_index("gy")),
        (2, lax.axis_size("gz"), 0, lax.axis_index("gz")),
    )
    context = (operator, fine_diagonal, shift_cells, row_totals, layout)
    residual = right_side
    smoothed = precondition(residual, context)
    gamma_now = total((jnp.sum(residual * smoothed),))[0]
    direction = smoothed
    image = fine_apply(direction, operator)
    step_size = gamma_now / total((jnp.sum(direction * image),))[0]
    solution_field = step_size * direction
    residual = residual - step_size * image
    smoothed = precondition(residual, context)
    gamma_next = total((jnp.sum(residual * smoothed),))[0]
    direction = smoothed + gamma_next / gamma_now * direction
    image = fine_apply(direction, operator)
    step_size = gamma_next / total((jnp.sum(direction * image),))[0]
    solution_field = solution_field + step_size * direction
    residual = residual - step_size * image
    return (solution_field, residual)


def solution(mesh):
    in_specs = (P("gx", "gy", "gz"), P("gx", "gy", "gz"), P(), P(), P())
    out_specs = (P("gx", "gy", "gz"), P("gx", "gy", "gz"))
    return jax.shard_map(
        per_device, mesh=mesh, in_specs=in_specs, out_specs=out_specs, check_vma=False
    )
```

profile of v0, /device:TPU:0, one launch (start us, length us, event | category | flops | bytes accessed | tf_op | source)
XLA Modules:
  0.0 322.8 jit_solution(2067341015985156474)
XLA Ops:
  4.0 4.9 %collective-permute-start.1 = (f32[1,2,8,64]{3,2,1,0:T(8,128)S(1)}, f32[1,2,8,64]{3,2,1,0:T(8,128)S(1)}, u32[]{:S(2)}, u32[]{:S(2)}) collective-permute-start(f32[1,2,8,64]{3,2,1,0:T(8,128)S(1)} %slice.578), channel_id=1, source_target_pairs={{0,16},{1,17},{2,18},{3,19},{4,20},{5,21},{6,22},{7,23},{8,24},{9,... | collective-permute-start | bytes 12296 | tf_op jit(solution)/shard_map/ppermute | solution.py:22
  18.8 4.5 %collective-permute-start.3 = (f32[6,1,8,64]{3,2,1,0:T(8,128)S(1)}, f32[6,1,8,64]{3,2,1,0:T(8,128)S(1)}, u32[]{:S(2)}, u32[]{:S(2)}) collective-permute-start(f32[6,1,8,64]{3,2,1,0:T(8,128)S(1)} %get-tuple-element.56), channel_id=1, source_target_pairs={{0,4},{4,8},{8,12},{1,5},{5,9},{9,13},{2,6},{6,10},{10,14},{3,7},{... | collective-permute-start | bytes 36872 | tf_op jit(solution)/shard_map/ppermute | solution.py:22
  27.6 3.4 %collective-permute-done.4 = f32[6,4,1,64]{3,2,1,0:T(1,128)S(1)} collective-permute-done((f32[6,4,1,64]{3,2,1,0:T(1,128)S(1)}, f32[6,4,1,64]{3,2,1,0:T(1,128)S(1)}, u32[]{:S(2)}, u32[]{:S(2)}) %collective-permute-start.4) | collective-permute-done | bytes 6176 | tf_op jit(solution)/shard_map/ppermute | solution.py:23
  31.9 2.7 collective-permute-start.6
  36.2 2.4 collective-permute-start.7
  42.3 2.8 collective-permute-start.9
  46.8 2.1 collective-permute-start.10
  52.7 3.9 %collective-permute-start.12 = (f32[1,2,8,64]{3,2,1,0:T(8,128)S(1)}, f32[1,2,8,64]{3,2,1,0:T(8,128)S(1)}, u32[]{:S(2)}, u32[]{:S(2)}) collective-permute-start(f32[1,2,8,64]{3,2,1,0:T(8,128)S(1)} %slice.631), channel_id=1, source_target_pairs={{0,16},{1,17},{2,18},{3,19},{4,20},{5,21},{6,22},{7,23},{8,24},{9,... | collective-permute-start | bytes 12296 | tf_op jit(solution)/shard_map/ppermute | solution.py:22
  58.2 4.2 %collective-permute-done.11 = f32[1,2,8,64]{3,2,1,0:T(8,128)S(1)} collective-permute-done((f32[1,2,8,64]{3,2,1,0:T(8,128)S(1)}, f32[1,2,8,64]{3,2,1,0:T(8,128)S(1)}, u32[]{:S(2)}, u32[]{:S(2)}) %collective-permute-start.11) | collective-permute-done | bytes 4128 | tf_op jit(solution)/shard_map/ppermute | solution.py:23
  63.7 4.5 %collective-permute-start.14 = (f32[6,1,8,64]{3,2,1,0:T(8,128)S(1)}, f32[6,1,8,64]{3,2,1,0:T(8,128)S(1)}, u32[]{:S(2)}, u32[]{:S(2)}) collective-permute-start(f32[6,1,8,64]{3,2,1,0:T(8,128)S(1)} %get-tuple-element.54), channel_id=1, source_target_pairs={{0,4},{4,8},{8,12},{1,5},{5,9},{9,13},{2,6},{6,10},{10,14},{3,7},{... | collective-permute-start | bytes 36872 | tf_op jit(solution)/shard_map/ppermute | solution.py:22
  73.2 3.3 %collective-permute-done.15 = f32[6,4,1,64]{3,2,1,0:T(1,128)S(1)} collective-permute-done((f32[6,4,1,64]{3,2,1,0:T(1,128)S(1)}, f32[6,4,1,64]{3,2,1,0:T(1,128)S(1)}, u32[]{:S(2)}, u32[]{:S(2)}) %collective-permute-start.15) | collective-permute-done | bytes 6176 | tf_op jit(solution)/shard_map/ppermute | solution.py:23
  80.4 4.2 %collective-permute-done.17 = f32[1,2,8,64]{3,2,1,0:T(8,128)S(1)} collective-permute-done((f32[1,2,8,64]{3,2,1,0:T(8,128)S(1)}, f32[1,2,8,64]{3,2,1,0:T(8,128)S(1)}, u32[]{:S(2)}, u32[]{:S(2)}) %collective-permute-start.17) | collective-permute-done | bytes 4128 | tf_op jit(solution)/shard_map/ppermute | solution.py:23
  85.9 4.7 %collective-permute-start.20 = (f32[6,1,8,64]{3,2,1,0:T(8,128)S(1)}, f32[6,1,8,64]{3,2,1,0:T(8,128)S(1)}, u32[]{:S(2)}, u32[]{:S(2)}) collective-permute-start(f32[6,1,8,64]{3,2,1,0:T(8,128)S(1)} %get-tuple-element.52), channel_id=1, source_target_pairs={{0,4},{4,8},{8,12},{1,5},{5,9},{9,13},{2,6},{6,10},{10,14},{3,7},{... | collective-permute-start | bytes 36872 | tf_op jit(solution)/shard_map/ppermute | solution.py:22
  92.3 2.6 collective-permute-start.22
  96.9 2.3 collective-permute-done.21
  100.4 41.2 %all-reduce.15 = (f32[]{:T(128)}, f32[]{:T(128)}) all-reduce(f32[]{:T(128)} %get-tuple-element.3, f32[]{:T(128)} %get-tuple-element.2), channel_id=1, replica_groups=mesh['gx'=2,'gy'=4,'gz'=4] {'gx','gy','gz'}, use_global_device_ids=true, to_apply=%region_13.14 | all-reduce | flops 2 | bytes 16 | tf_op jit(solution)/shard_map/psum | solution.py:157
  143.0 4.4 %collective-permute-start.24 = (f32[1,2,8,64]{3,2,1,0:T(8,128)S(1)}, f32[1,2,8,64]{3,2,1,0:T(8,128)S(1)}, u32[]{:S(2)}, u32[]{:S(2)}) collective-permute-start(f32[1,2,8,64]{3,2,1,0:T(8,128)S(1)} %slice.659), channel_id=1, source_target_pairs={{0,16},{1,17},{2,18},{3,19},{4,20},{5,21},{6,22},{7,23},{8,24},{9,... | collective-permute-start | bytes 12296 | tf_op jit(solution)/shard_map/ppermute | solution.py:22
  149.0 4.2 %collective-permute-done.23 = f32[1,2,8,64]{3,2,1,0:T(8,128)S(1)} collective-permute-done((f32[1,2,8,64]{3,2,1,0:T(8,128)S(1)}, f32[1,2,8,64]{3,2,1,0:T(8,128)S(1)}, u32[]{:S(2)}, u32[]{:S(2)}) %collective-permute-start.23) | collective-permute-done | bytes 4128 | tf_op jit(solution)/shard_map/ppermute | solution.py:23
  154.5 4.7 %collective-permute-start.26 = (f32[6,1,8,64]{3,2,1,0:T(8,128)S(1)}, f32[6,1,8,64]{3,2,1,0:T(8,128)S(1)}, u32[]{:S(2)}, u32[]{:S(2)}) collective-permute-start(f32[6,1,8,64]{3,2,1,0:T(8,128)S(1)} %get-tuple-element.50), channel_id=1, source_target_pairs={{0,4},{4,8},{8,12},{1,5},{5,9},{9,13},{2,6},{6,10},{10,14},{3,7},{... | collective-permute-start | bytes 36872 | tf_op jit(solution)/shard_map/ppermute | solution.py:22
  164.2 3.3 %collective-permute-done.27 = f32[6,4,1,64]{3,2,1,0:T(1,128)S(1)} collective-permute-done((f32[6,4,1,64]{3,2,1,0:T(1,128)S(1)}, f32[6,4,1,64]{3,2,1,0:T(1,128)S(1)}, u32[]{:S(2)}, u32[]{:S(2)}) %collective-permute-start.27) | collective-permute-done | bytes 6176 | tf_op jit(solution)/shard_map/ppermute | solution.py:23
  168.5 3.6 %collective-permute-done.29 = f32[2,2,1,4]{3,1,2,0:T(2,128)S(1)} collective-permute-done((f32[2,2,1,4]{3,1,2,0:T(2,128)S(1)}, f32[2,2,1,4]{3,1,2,0:T(2,128)S(1)}, u32[]{:S(2)}, u32[]{:S(2)}) %collective-permute-start.29) | collective-permute-done | bytes 96 | tf_op jit(solution)/shard_map/ppermute | solution.py:29
  177.6 3.4 %collective-permute-start.32 = (f32[2,2,1,4]{3,1,2,0:T(2,128)S(1)}, f32[2,2,1,4]{3,1,2,0:T(2,128)S(1)}, u32[]{:S(2)}, u32[]{:S(2)}) collective-permute-start(f32[2,2,1,4]{3,1,2,0:T(2,128)S(1)} %pad_maximum_fusion.85), channel_id=1, source_target_pairs={{0,8},{1,9},{2,10},{3,11},{4,12},{5,13},{6,14},{7,15},{8,0},{9,1},... | collective-permute-start | bytes 200 | tf_op jit(solution)/shard_map/ppermute | solution.py:29
  182.5 2.4 collective-permute-start.33
  192.1 4.2 %collective-permute-done.34 = f32[1,2,8,64]{3,2,1,0:T(8,128)S(1)} collective-permute-done((f32[1,2,8,64]{3,2,1,0:T(8,128)S(1)}, f32[1,2,8,64]{3,2,1,0:T(8,128)S(1)}, u32[]{:S(2)}, u32[]{:S(2)}) %collective-permute-start.34) | collective-permute-done | bytes 4128 | tf_op jit(solution)/shard_map/ppermute | solution.py:23
  197.6 4.5 %collective-permute-start.37 = (f32[6,1,8,64]{3,2,1,0:T(8,128)S(1)}, f32[6,1,8,64]{3,2,1,0:T(8,128)S(1)}, u32[]{:S(2)}, u32[]{:S(2)}) collective-permute-start(f32[6,1,8,64]{3,2,1,0:T(8,128)S(1)} %get-tuple-element.48), channel_id=1, source_target_pairs={{0,4},{4,8},{8,12},{1,5},{5,9},{9,13},{2,6},{6,10},{10,14},{3,7},{... | collective-permute-start | bytes 36872 | tf_op jit(solution)/shard_map/ppermute | solution.py:22
  207.1 3.3 %collective-permute-done.38 = f32[6,4,1,64]{3,2,1,0:T(1,128)S(1)} collective-permute-done((f32[6,4,1,64]{3,2,1,0:T(1,128)S(1)}, f32[6,4,1,64]{3,2,1,0:T(1,128)S(1)}, u32[]{:S(2)}, u32[]{:S(2)}) %collective-permute-start.38) | collective-permute-done | bytes 6176 | tf_op jit(solution)/shard_map/ppermute | solution.py:23
  211.6 40.7 %psum.30 = f32[]{:T(128)} all-reduce(f32[]{:T(128)} %get-tuple-element.6), channel_id=1, replica_groups=mesh['gx'=2,'gy'=4,'gz'=4] {'gx','gy','gz'}, use_global_device_ids=true, to_apply=%region_28.29 | all-reduce | flops 1 | bytes 8 | tf_op jit(solution)/shard_map/psum | solution.py:157
  253.7 4.4 %collective-permute-start.41 = (f32[1,2,8,64]{3,2,1,0:T(8,128)S(1)}, f32[1,2,8,64]{3,2,1,0:T(8,128)S(1)}, u32[]{:S(2)}, u32[]{:S(2)}) collective-permute-start(f32[1,2,8,64]{3,2,1,0:T(8,128)S(1)} %slice.721), channel_id=1, source_target_pairs={{0,16},{1,17},{2,18},{3,19},{4,20},{5,21},{6,22},{7,23},{8,24},{9,... | collective-permute-start | bytes 12296 | tf_op jit(solution)/shard_map/ppermute | solution.py:22
  259.7 4.2 %collective-permute-done.40 = f32[1,2,8,64]{3,2,1,0:T(8,128)S(1)} collective-permute-done((f32[1,2,8,64]{3,2,1,0:T(8,128)S(1)}, f32[1,2,8,64]{3,2,1,0:T(8,128)S(1)}, u32[]{:S(2)}, u32[]{:S(2)}) %collective-permute-start.40) | collective-permute-done | bytes 4128 | tf_op jit(solution)/shard_map/ppermute | solution.py:23
  265.2 4.5 %collective-permute-start.43 = (f32[6,1,8,64]{3,2,1,0:T(8,128)S(1)}, f32[6,1,8,64]{3,2,1,0:T(8,128)S(1)}, u32[]{:S(2)}, u32[]{:S(2)}) collective-permute-start(f32[6,1,8,64]{3,2,1,0:T(8,128)S(1)} %get-tuple-element.46), channel_id=1, source_target_pairs={{0,4},{4,8},{8,12},{1,5},{5,9},{9,13},{2,6},{6,10},{10,14},{3,7},{... | collective-permute-start | bytes 36872 | tf_op jit(solution)/shard_map/ppermute | solution.py:22
  274.7 3.3 %collective-permute-done.44 = f32[6,4,1,64]{3,2,1,0:T(1,128)S(1)} collective-permute-done((f32[6,4,1,64]{3,2,1,0:T(1,128)S(1)}, f32[6,4,1,64]{3,2,1,0:T(1,128)S(1)}, u32[]{:S(2)}, u32[]{:S(2)}) %collective-permute-start.44) | collective-permute-done | bytes 6176 | tf_op jit(solution)/shard_map/ppermute | solution.py:23
  279.1 41.1 %psum.31 = f32[]{:T(128)} all-reduce(f32[]{:T(128)} %multiply_reduce_fusion), channel_id=1, replica_groups=mesh['gx'=2,'gy'=4,'gz'=4] {'gx','gy','gz'}, use_global_device_ids=true, to_apply=%region_30.31 | all-reduce | flops 1 | bytes 8 | tf_op jit(solution)/shard_map/psum | solution.py:157
  (321 shorter events, 86.6 us)
Async XLA Ops:
  4.0 13.5 %collective-permute-start.1 = (f32[1,2,8,64]{3,2,1,0:T(8,128)S(1)}, f32[1,2,8,64]{3,2,1,0:T(8,128)S(1)}, u32[]{:S(2)}, u32[]{:S(2)}) collective-permute-start(f32[1,2,8,64]{3,2,1,0:T(8,128)S(1)} %slice.578), channel_id=1, source_target_pairs={{0,16},{1,17},{2,18},{3,19},{4,20},{5,21},{6,22},{7,23},{8,24},{9,... | collective-permute-start | bytes 12296 | tf_op jit(solution)/shard_map/ppermute | solution.py:22
  8.9 8.6 %collective-permute-start = (f32[1,2,8,64]{3,2,1,0:T(8,128)S(1)}, f32[1,2,8,64]{3,2,1,0:T(8,128)S(1)}, u32[]{:S(2)}, u32[]{:S(2)}) collective-permute-start(f32[1,2,8,64]{3,2,1,0:T(8,128)S(1)} %slice.575), channel_id=1, source_target_pairs={{16,0},{17,1},{18,2},{19,3},{20,4},{21,5},{22,6},{23,7},{24,8},{25... | collective-permute-start | bytes 12296 | tf_op jit(solution)/shard_map/ppermute | solution.py:23
  17.5 7.0 %collective-permute-start.2 = (f32[6,1,8,64]{3,2,1,0:T(8,128)S(1)}, f32[6,1,8,64]{3,2,1,0:T(8,128)S(1)}, u32[]{:S(2)}, u32[]{:S(2)}) collective-permute-start(f32[6,1,8,64]{3,2,1,0:T(8,128)S(1)} %get-tuple-element.57), channel_id=1, source_target_pairs={{4,0},{8,4},{12,8},{5,1},{9,5},{13,9},{6,2},{10,6},{14,10},{7,3},{... | collective-permute-start | bytes 36872 | tf_op jit(solution)/shard_map/ppermute | solution.py:23
  18.8 6.1 %collective-permute-start.3 = (f32[6,1,8,64]{3,2,1,0:T(8,128)S(1)}, f32[6,1,8,64]{3,2,1,0:T(8,128)S(1)}, u32[]{:S(2)}, u32[]{:S(2)}) collective-permute-start(f32[6,1,8,64]{3,2,1,0:T(8,128)S(1)} %get-tuple-element.56), channel_id=1, source_target_pairs={{0,4},{4,8},{8,12},{1,5},{5,9},{9,13},{2,6},{6,10},{10,14},{3,7},{... | collective-permute-start | bytes 36872 | tf_op jit(solution)/shard_map/ppermute | solution.py:22
  26.2 4.8 %collective-permute-start.4 = (f32[6,4,1,64]{3,2,1,0:T(1,128)S(1)}, f32[6,4,1,64]{3,2,1,0:T(1,128)S(1)}, u32[]{:S(2)}, u32[]{:S(2)}) collective-permute-start(f32[6,4,1,64]{3,2,1,0:T(1,128)S(1)} %get-tuple-element.33), channel_id=1, source_target_pairs={{1,0},{2,1},{3,2},{5,4},{6,5},{7,6},{9,8},{10,9},{11,10},{13,12},{... | collective-permute-start | bytes 18440 | tf_op jit(solution)/shard_map/ppermute | solution.py:23
  31.9 4.3 %collective-permute-start.6 = (f32[2,2,1,4]{3,1,2,0:T(2,128)S(1)}, f32[2,2,1,4]{3,1,2,0:T(2,128)S(1)}, u32[]{:S(2)}, u32[]{:S(2)}) collective-permute-start(f32[2,2,1,4]{3,1,2,0:T(2,128)S(1)} %pad_maximum_fusion.83), channel_id=1, source_target_pairs={{0,16},{1,17},{2,18},{3,19},{4,20},{5,21},{6,22},{7,23},{8,24},{9,... | collective-permute-start | bytes 200 | tf_op jit(solution)/shard_map/ppermute | solution.py:29
  42.3 4.5 %collective-permute-start.9 = (f32[2,2,1,4]{3,1,2,0:T(2,128)S(1)}, f32[2,2,1,4]{3,1,2,0:T(2,128)S(1)}, u32[]{:S(2)}, u32[]{:S(2)}) collective-permute-start(f32[2,2,1,4]{3,1,2,0:T(2,128)S(1)} %pad_maximum_fusion.84), channel_id=1, source_target_pairs={{0,8},{1,9},{2,10},{3,11},{4,12},{5,13},{6,14},{7,15},{8,0},{9,1},... | collective-permute-start | bytes 200 | tf_op jit(solution)/shard_map/ppermute | solution.py:29
  52.7 5.5 %collective-permute-start.12 = (f32[1,2,8,64]{3,2,1,0:T(8,128)S(1)}, f32[1,2,8,64]{3,2,1,0:T(8,128)S(1)}, u32[]{:S(2)}, u32[]{:S(2)}) collective-permute-start(f32[1,2,8,64]{3,2,1,0:T(8,128)S(1)} %slice.631), channel_id=1, source_target_pairs={{0,16},{1,17},{2,18},{3,19},{4,20},{5,21},{6,22},{7,23},{8,24},{9,... | collective-permute-start | bytes 12296 | tf_op jit(solution)/shard_map/ppermute | solution.py:22
  56.8 5.5 %collective-permute-start.11 = (f32[1,2,8,64]{3,2,1,0:T(8,128)S(1)}, f32[1,2,8,64]{3,2,1,0:T(8,128)S(1)}, u32[]{:S(2)}, u32[]{:S(2)}) collective-permute-start(f32[1,2,8,64]{3,2,1,0:T(8,128)S(1)} %slice.628), channel_id=1, source_target_pairs={{16,0},{17,1},{18,2},{19,3},{20,4},{21,5},{22,6},{23,7},{24,8},{25... | collective-permute-start | bytes 12296 | tf_op jit(solution)/shard_map/ppermute | solution.py:23
  62.4 7.5 %collective-permute-start.13 = (f32[6,1,8,64]{3,2,1,0:T(8,128)S(1)}, f32[6,1,8,64]{3,2,1,0:T(8,128)S(1)}, u32[]{:S(2)}, u32[]{:S(2)}) collective-permute-start(f32[6,1,8,64]{3,2,1,0:T(8,128)S(1)} %get-tuple-element.55), channel_id=1, source_target_pairs={{4,0},{8,4},{12,8},{5,1},{9,5},{13,9},{6,2},{10,6},{14,10},{7,3},{... | collective-permute-start | bytes 36872 | tf_op jit(solution)/shard_map/ppermute | solution.py:23
  63.7 6.2 %collective-permute-start.14 = (f32[6,1,8,64]{3,2,1,0:T(8,128)S(1)}, f32[6,1,8,64]{3,2,1,0:T(8,128)S(1)}, u32[]{:S(2)}, u32[]{:S(2)}) collective-permute-start(f32[6,1,8,64]{3,2,1,0:T(8,128)S(1)} %get-tuple-element.54), channel_id=1, source_target_pairs={{0,4},{4,8},{8,12},{1,5},{5,9},{9,13},{2,6},{6,10},{10,14},{3,7},{... | collective-permute-start | bytes 36872 | tf_op jit(solution)/shard_map/ppermute | solution.py:22
  71.2 5.3 %collective-permute-start.15 = (f32[6,4,1,64]{3,2,1,0:T(1,128)S(1)}, f32[6,4,1,64]{3,2,1,0:T(1,128)S(1)}, u32[]{:S(2)}, u32[]{:S(2)}) collective-permute-start(f32[6,4,1,64]{3,2,1,0:T(1,128)S(1)} %get-tuple-element.29), channel_id=1, source_target_pairs={{1,0},{2,1},{3,2},{5,4},{6,5},{7,6},{9,8},{10,9},{11,10},{13,12},{... | collective-permute-start | bytes 18440 | tf_op jit(solution)/shard_map/ppermute | solution.py:23
  79.1 5.5 %collective-permute-start.17 = (f32[1,2,8,64]{3,2,1,0:T(8,128)S(1)}, f32[1,2,8,64]{3,2,1,0:T(8,128)S(1)}, u32[]{:S(2)}, u32[]{:S(2)}) collective-permute-start(f32[1,2,8,64]{3,2,1,0:T(8,128)S(1)} %slice.642), channel_id=1, source_target_pairs={{16,0},{17,1},{18,2},{19,3},{20,4},{21,5},{22,6},{23,7},{24,8},{25... | collective-permute-start | bytes 12296 | tf_op jit(solution)/shard_map/ppermute | solution.py:23
  84.6 7.6 %collective-permute-start.19 = (f32[6,1,8,64]{3,2,1,0:T(8,128)S(1)}, f32[6,1,8,64]{3,2,1,0:T(8,128)S(1)}, u32[]{:S(2)}, u32[]{:S(2)}) collective-permute-start(f32[6,1,8,64]{3,2,1,0:T(8,128)S(1)} %get-tuple-element.53), channel_id=1, source_target_pairs={{4,0},{8,4},{12,8},{5,1},{9,5},{13,9},{6,2},{10,6},{14,10},{7,3},{... | collective-permute-start | bytes 36872 | tf_op jit(solution)/shard_map/ppermute | solution.py:23
  85.9 6.3 %collective-permute-start.20 = (f32[6,1,8,64]{3,2,1,0:T(8,128)S(1)}, f32[6,1,8,64]{3,2,1,0:T(8,128)S(1)}, u32[]{:S(2)}, u32[]{:S(2)}) collective-permute-start(f32[6,1,8,64]{3,2,1,0:T(8,128)S(1)} %get-tuple-element.52), channel_id=1, source_target_pairs={{0,4},{4,8},{8,12},{1,5},{5,9},{9,13},{2,6},{6,10},{10,14},{3,7},{... | collective-permute-start | bytes 36872 | tf_op jit(solution)/shard_map/ppermute | solution.py:22
  92.3 4.6 %collective-permute-start.22 = (f32[6,4,1,64]{3,2,1,0:T(1,128)S(1)}, f32[6,4,1,64]{3,2,1,0:T(1,128)S(1)}, u32[]{:S(2)}, u32[]{:S(2)}) collective-permute-start(f32[6,4,1,64]{3,2,1,0:T(1,128)S(1)} %get-tuple-element.24), channel_id=1, source_target_pairs={{0,1},{1,2},{2,3},{4,5},{5,6},{6,7},{8,9},{9,10},{10,11},{12,13},{... | collective-permute-start | bytes 18440 | tf_op jit(solution)/shard_map/ppermute | solution.py:22
  94.9 4.3 %collective-permute-start.21 = (f32[6,4,1,64]{3,2,1,0:T(1,128)S(1)}, f32[6,4,1,64]{3,2,1,0:T(1,128)S(1)}, u32[]{:S(2)}, u32[]{:S(2)}) collective-permute-start(f32[6,4,1,64]{3,2,1,0:T(1,128)S(1)} %get-tuple-element.25), channel_id=1, source_target_pairs={{1,0},{2,1},{3,2},{5,4},{6,5},{7,6},{9,8},{10,9},{11,10},{13,12},{... | collective-permute-start | bytes 18440 | tf_op jit(solution)/shard_map/ppermute | solution.py:23
  143.0 5.9 %collective-permute-start.24 = (f32[1,2,8,64]{3,2,1,0:T(8,128)S(1)}, f32[1,2,8,64]{3,2,1,0:T(8,128)S(1)}, u32[]{:S(2)}, u32[]{:S(2)}) collective-permute-start(f32[1,2,8,64]{3,2,1,0:T(8,128)S(1)} %slice.659), channel_id=1, source_target_pairs={{0,16},{1,17},{2,18},{3,19},{4,20},{5,21},{6,22},{7,23},{8,24},{9,... | collective-permute-start | bytes 12296 | tf_op jit(solution)/shard_map/ppermute | solution.py:22
  147.7 5.5 %collective-permute-start.23 = (f32[1,2,8,64]{3,2,1,0:T(8,128)S(1)}, f32[1,2,8,64]{3,2,1,0:T(8,128)S(1)}, u32[]{:S(2)}, u32[]{:S(2)}) collective-permute-start(f32[1,2,8,64]{3,2,1,0:T(8,128)S(1)} %slice.656), channel_id=1, source_target_pairs={{16,0},{17,1},{18,2},{19,3},{20,4},{21,5},{22,6},{23,7},{24,8},{25... | collective-permute-start | bytes 12296 | tf_op jit(solution)/shard_map/ppermute | solution.py:23
  153.2 7.6 %collective-permute-start.25 = (f32[6,1,8,64]{3,2,1,0:T(8,128)S(1)}, f32[6,1,8,64]{3,2,1,0:T(8,128)S(1)}, u32[]{:S(2)}, u32[]{:S(2)}) collective-permute-start(f32[6,1,8,64]{3,2,1,0:T(8,128)S(1)} %get-tuple-element.51), channel_id=1, source_target_pairs={{4,0},{8,4},{12,8},{5,1},{9,5},{13,9},{6,2},{10,6},{14,10},{7,3},{... | collective-permute-start | bytes 36872 | tf_op jit(solution)/shard_map/ppermute | solution.py:23
  154.5 6.4 %collective-permute-start.26 = (f32[6,1,8,64]{3,2,1,0:T(8,128)S(1)}, f32[6,1,8,64]{3,2,1,0:T(8,128)S(1)}, u32[]{:S(2)}, u32[]{:S(2)}) collective-permute-start(f32[6,1,8,64]{3,2,1,0:T(8,128)S(1)} %get-tuple-element.50), channel_id=1, source_target_pairs={{0,4},{4,8},{8,12},{1,5},{5,9},{9,13},{2,6},{6,10},{10,14},{3,7},{... | collective-permute-start | bytes 36872 | tf_op jit(solution)/shard_map/ppermute | solution.py:22
  162.2 5.3 %collective-permute-start.27 = (f32[6,4,1,64]{3,2,1,0:T(1,128)S(1)}, f32[6,4,1,64]{3,2,1,0:T(1,128)S(1)}, u32[]{:S(2)}, u32[]{:S(2)}) collective-permute-start(f32[6,4,1,64]{3,2,1,0:T(1,128)S(1)} %get-tuple-element.21), channel_id=1, source_target_pairs={{1,0},{2,1},{3,2},{5,4},{6,5},{7,6},{9,8},{10,9},{11,10},{13,12},{... | collective-permute-start | bytes 18440 | tf_op jit(solution)/shard_map/ppermute | solution.py:23
  177.6 4.9 %collective-permute-start.32 = (f32[2,2,1,4]{3,1,2,0:T(2,128)S(1)}, f32[2,2,1,4]{3,1,2,0:T(2,128)S(1)}, u32[]{:S(2)}, u32[]{:S(2)}) collective-permute-start(f32[2,2,1,4]{3,1,2,0:T(2,128)S(1)} %pad_maximum_fusion.85), channel_id=1, source_target_pairs={{0,8},{1,9},{2,10},{3,11},{4,12},{5,13},{6,14},{7,15},{8,0},{9,1},... | collective-permute-start | bytes 200 | tf_op jit(solution)/shard_map/ppermute | solution.py:29
  190.8 5.5 %collective-permute-start.34 = (f32[1,2,8,64]{3,2,1,0:T(8,128)S(1)}, f32[1,2,8,64]{3,2,1,0:T(8,128)S(1)}, u32[]{:S(2)}, u32[]{:S(2)}) collective-permute-start(f32[1,2,8,64]{3,2,1,0:T(8,128)S(1)} %slice.704), channel_id=1, source_target_pairs={{16,0},{17,1},{18,2},{19,3},{20,4},{21,5},{22,6},{23,7},{24,8},{25... | collective-permute-start | bytes 12296 | tf_op jit(solution)/shard_map/ppermute | solution.py:23
  196.3 7.5 %collective-permute-start.36 = (f32[6,1,8,64]{3,2,1,0:T(8,128)S(1)}, f32[6,1,8,64]{3,2,1,0:T(8,128)S(1)}, u32[]{:S(2)}, u32[]{:S(2)}) collective-permute-start(f32[6,1,8,64]{3,2,1,0:T(8,128)S(1)} %get-tuple-element.49), channel_id=1, source_target_pairs={{4,0},{8,4},{12,8},{5,1},{9,5},{13,9},{6,2},{10,6},{14,10},{7,3},{... | collective-permute-start | bytes 36872 | tf_op jit(solution)/shard_map/ppermute | solution.py:23
  197.6 6.2 %collective-permute-start.37 = (f32[6,1,8,64]{3,2,1,0:T(8,128)S(1)}, f32[6,1,8,64]{3,2,1,0:T(8,128)S(1)}, u32[]{:S(2)}, u32[]{:S(2)}) collective-permute-start(f32[6,1,8,64]{3,2,1,0:T(8,128)S(1)} %get-tuple-element.48), channel_id=1, source_target_pairs={{0,4},{4,8},{8,12},{1,5},{5,9},{9,13},{2,6},{6,10},{10,14},{3,7},{... | collective-permute-start | bytes 36872 | tf_op jit(solution)/shard_map/ppermute | solution.py:22
  205.1 5.3 %collective-permute-start.38 = (f32[6,4,1,64]{3,2,1,0:T(1,128)S(1)}, f32[6,4,1,64]{3,2,1,0:T(1,128)S(1)}, u32[]{:S(2)}, u32[]{:S(2)}) collective-permute-start(f32[6,4,1,64]{3,2,1,0:T(1,128)S(1)} %get-tuple-element.17), channel_id=1, source_target_pairs={{1,0},{2,1},{3,2},{5,4},{6,5},{7,6},{9,8},{10,9},{11,10},{13,12},{... | collective-permute-start | bytes 18440 | tf_op jit(solution)/shard_map/ppermute | solution.py:23
  253.7 5.9 %collective-permute-start.41 = (f32[1,2,8,64]{3,2,1,0:T(8,128)S(1)}, f32[1,2,8,64]{3,2,1,0:T(8,128)S(1)}, u32[]{:S(2)}, u32[]{:S(2)}) collective-permute-start(f32[1,2,8,64]{3,2,1,0:T(8,128)S(1)} %slice.721), channel_id=1, source_target_pairs={{0,16},{1,17},{2,18},{3,19},{4,20},{5,21},{6,22},{7,23},{8,24},{9,... | collective-permute-start | bytes 12296 | tf_op jit(solution)/shard_map/ppermute | solution.py:22
  258.4 5.5 %collective-permute-start.40 = (f32[1,2,8,64]{3,2,1,0:T(8,128)S(1)}, f32[1,2,8,64]{3,2,1,0:T(8,128)S(1)}, u32[]{:S(2)}, u32[]{:S(2)}) collective-permute-start(f32[1,2,8,64]{3,2,1,0:T(8,128)S(1)} %slice.718), channel_id=1, source_target_pairs={{16,0},{17,1},{18,2},{19,3},{20,4},{21,5},{22,6},{23,7},{24,8},{25... | collective-permute-start | bytes 12296 | tf_op jit(solution)/shard_map/ppermute | solution.py:23
  263.9 7.5 %collective-permute-start.42 = (f32[6,1,8,64]{3,2,1,0:T(8,128)S(1)}, f32[6,1,8,64]{3,2,1,0:T(8,128)S(1)}, u32[]{:S(2)}, u32[]{:S(2)}) collective-permute-start(f32[6,1,8,64]{3,2,1,0:T(8,128)S(1)} %get-tuple-element.47), channel_id=1, source_target_pairs={{4,0},{8,4},{12,8},{5,1},{9,5},{13,9},{6,2},{10,6},{14,10},{7,3},{... | collective-permute-start | bytes 36872 | tf_op jit(solution)/shard_map/ppermute | solution.py:23
  265.2 6.2 %collective-permute-start.43 = (f32[6,1,8,64]{3,2,1,0:T(8,128)S(1)}, f32[6,1,8,64]{3,2,1,0:T(8,128)S(1)}, u32[]{:S(2)}, u32[]{:S(2)}) collective-permute-start(f32[6,1,8,64]{3,2,1,0:T(8,128)S(1)} %get-tuple-element.46), channel_id=1, source_target_pairs={{0,4},{4,8},{8,12},{1,5},{5,9},{9,13},{2,6},{6,10},{10,14},{3,7},{... | collective-permute-start | bytes 36872 | tf_op jit(solution)/shard_map/ppermute | solution.py:22
  272.7 5.3 %collective-permute-start.44 = (f32[6,4,1,64]{3,2,1,0:T(1,128)S(1)}, f32[6,4,1,64]{3,2,1,0:T(1,128)S(1)}, u32[]{:S(2)}, u32[]{:S(2)}) collective-permute-start(f32[6,4,1,64]{3,2,1,0:T(1,128)S(1)} %get-tuple-element.13), channel_id=1, source_target_pairs={{1,0},{2,1},{3,2},{5,4},{6,5},{7,6},{9,8},{10,9},{11,10},{13,12},{... | collective-permute-start | bytes 18440 | tf_op jit(solution)/shard_map/ppermute | solution.py:23
  (25 other events, 178.7 us)
where the time goes:
time: 324 us; the launch traced here: 323 us
  blocking collectives  123 us (38%)
  starting transfers between devices  99.9 us (31%)
  waiting for transfers between devices  57 us (18%)
  matrix products  16.6 us (5%)
  other arithmetic  11.1 us (3%)
  local copies, waits for them, and re-layouts  9.31 us (3%)
  between operations  5.99 us (2%)
    psum x3, blocking collectives, total(): return lax.psum(terms, ('gx', 'gy', 'gz'))  123 us
    ppermute x18, starting transfers between devices, with_halo(): before = lax.ppermute(last, axis, up)  57.8 us
    ppermute x18, waiting for transfers between devices, with_halo(): after = lax.ppermute(first, axis, down)  40.2 us
    ppermute x18, starting transfers between devices, with_halo(): after = lax.ppermute(first, axis, down)  23.2 us
    ppermute x10, starting transfers between devices, partner_2(): lax.ppermute(x, axis, [(i, i ^ 1 << bit) for i in range(lax.axis_size(axi...  19 us
    ppermute x10, waiting for transfers between devices, partner_2(): lax.ppermute(x, axis, [(i, i ^ 1 << bit) for i in range(lax.axis_size(axi...  16.4 us
    dot_general x6, matrix products, fine_apply(): jnp.dot(flat, wide_blocks, precision=highest)  9.65 us
  transfers between devices with their start and end apart: 46, of which 22 were waited for; matrix products, arithmetic and copies ran while one was open for 7% of the time, Pallas kernels for 0%

commit v1 on v0

--- a/solution.py
+++ b/solution.py
@@ -2,6 +2,8 @@
 import jax.numpy as jnp
 import numpy as np
 from jax import lax
+from jax.experimental import pallas as pl
+from jax.experimental.pallas import tpu as pltpu
 from jax.sharding import PartitionSpec as P
 
 P_SIZE = 64
@@ -199,9 +201,379 @@
     return (solution_field, residual)
 
 
+AXES = (2, 4, 4)
+DEVICES = 32
+CELLS = 256
+MESSAGE = 384
+HALO_ROUNDS = 4
+MESH = pl.DeviceIdType.MESH
+f32 = jnp.float32
+
+
+def iota(shape, dim):
+    return lax.broadcasted_iota(jnp.int32, shape, dim)
+
+
+def exact_dot(a, b):
+    return jnp.dot(a, b, precision=highest, preferred_element_type=f32)
+
+
+def neighbours(count, bits_y, bits_z, section_y, section_z):
+    i, j = iota((count, count), 0), iota((count, count), 1)
+
+    def split(k):
+        return k >> bits_y + bits_z, k >> bits_z & (1 << bits_y) - 1, k & (1 << bits_z) - 1
+
+    (xi, yi, zi), (xj, yj, zj) = split(i), split(j)
+    apart = jnp.abs(xi - xj) + jnp.abs(yi - yj) + jnp.abs(zi - zj)
+    same = ((yi >> section_y) == (yj >> section_y)) & ((zi >> section_z) == (zj >> section_z))
+    return jnp.where((apart == 1) & same, 1.0, 0.0).astype(f32)
+
+
+def coarse_matrix(shift_row):
+    i, j = iota((CELLS, CELLS), 0), iota((CELLS, CELLS), 1)
+    eye = jnp.where(i == j, 1.0, 0.0).astype(f32)
+    beside_1 = neighbours(CELLS, 2, 4, 1, 3)
+    beside_2 = neighbours(32, 1, 3, 1, 3)
+    j2, cell = iota((32, CELLS), 0), iota((32, CELLS), 1)
+    parent = (cell >> 7) * 16 + (cell >> 5 & 1) * 8 + (cell >> 1 & 7)
+    down_1 = jnp.where(parent == j2, 1.0, 0.0).astype(f32)
+    ci, cj = iota((CELLS, 32), 0), iota((CELLS, 32), 1)
+    up_1 = jnp.where((ci >> 7) * 16 + (ci >> 5 & 1) * 8 + (ci >> 1 & 7) == cj, 1.0, 0.0).astype(f32)
+    j3, k3 = iota((8, 32), 0), iota((8, 32), 1)
+    down_2 = jnp.where((k3 >> 1 & 3) == j3, 1.0, 0.0).astype(f32)
+    k2, i2 = iota((32, 8), 0), iota((32, 8), 1)
+    up_2 = jnp.where((k2 >> 1 & 3) == i2, 1.0, 0.0).astype(f32)
+    d1_row = 6.0 + shift_row
+    d1 = jnp.sum(eye * d1_row, axis=1, keepdims=True)
+    d2 = 6.0 + 0.125 * jnp.sum(down_1 * shift_row, axis=1, keepdims=True)
+    j3w, cellw = iota((8, CELLS), 0), iota((8, CELLS), 1)
+    d3 = 6.0 + 0.015625 * jnp.sum(
+        jnp.where((cellw >> 2 & 3) == j3w, shift_row, 0.0), axis=1, keepdims=True
+    )
+    q2 = 0.25 * exact_dot(down_1, 0.4 * eye + 0.6 * beside_1 / d1_row)
+    x2 = 0.6 * q2 / d2
+    q3 = 0.25 * exact_dot(down_2, 0.4 * q2 + exact_dot(beside_2, x2))
+    x3 = 0.6 * q3 / d3
+    row = iota((8, CELLS), 0)
+    for _ in range(SWEEPS - 1):
+        after = jnp.where(row < 3, pltpu.roll(x3, 7, 0), 0.0)
+        before = jnp.where((row > 0) & (row < 4), pltpu.roll(x3, 1, 0), 0.0)
+        x3 = 0.4 * x3 + 0.6 * (q3 + after + before) / d3
+    x2 = x2 + exact_dot(up_2, x3)
+    x2 = 0.4 * x2 + 0.6 * (q2 + exact_dot(beside_2, x2)) / d2
+    x1 = 0.6 * eye / d1 + exact_dot(up_1, x2)
+    return 0.4 * x1 + 0.6 * (eye + exact_dot(beside_1, x1)) / d1
+
+
+def pick_cells(gx, gy, gz):
+    rows = []
+    s, cell = iota((8, CELLS), 0), iota((8, CELLS), 1)
+    x, y = s >> 1, s & 1
+    cx, cy, cz = cell >> 6, cell >> 4 & 3, cell & 15
+    for dx, dy, zs in ((0, 0, range(-1, 5)), (1, 0, range(4)), (-1, 0, range(4)), (0, 1, range(4)), (0, -1, range(4))):
+        at_x = (gx * 4 + x + dx) >> 1
+        at_y = (gy * 2 + y + dy) >> 1
+        for z in zs:
+            hit = (cx == at_x) & (cy == at_y) & (cz == gz * 4 + z)
+            rows.append(jnp.where(hit, 1.0, 0.0).astype(f32))
+    return jnp.concatenate(rows, axis=0)
+
+
+def fused(
+    r_ref, class_ref, blocks_ref, shift_ref, weight_ref, x_out, r_out,
+    halo_out, halo_in, note_out, note_in, w_hi, w_lo, cells_ref,
+    halo_send, halo_recv, note_send, note_recv,
+):
+    gx, gy, gz = lax.axis_index("gx"), lax.axis_index("gy"), lax.axis_index("gz")
+    me = gx * 16 + gy * 4 + gz
+
+    def others(act):
+        def step(k, carry):
+            to = lax.rem(me + k, DEVICES)
+            act((to // 16, lax.rem(to // 4, 4), lax.rem(to, 4)))
+            return carry
+
+        lax.fori_loop(1, DEVICES, step, 0)
+
+    barrier = pltpu.get_barrier_semaphore()
+    halo_in[...] = jnp.zeros_like(halo_in)
+    others(lambda to: pl.semaphore_signal(barrier, inc=1, device_id=to, device_id_type=MESH))
+
+    lane = iota((8, 128), 1)
+    sub = iota((8, 128), 0)
+    low = lane < 64
+    ni, nj, nk = lane >> 4 & 3, lane >> 2 & 3, lane & 3
+    weights = [weight_ref[d] for d in range(3)]
+    upper = [jnp.where(n == 3, w, 0.0) for n, w in zip((ni, nj, nk), weights)]
+    lower = [jnp.where(n == 0, w, 0.0) for n, w in zip((ni, nj, nk), weights)]
+
+    def widen(blocks):
+        out = []
+        for j in range(4):
+            turned = pltpu.roll(blocks[j], 64, 1)
+            out += [jnp.where(low, blocks[j], turned), jnp.where(low, turned, blocks[j])]
+        return out
+
+    def halves(u):
+        return [jnp.where(low, u[2 * j], u[2 * j + 1]) for j in range(4)]
+
+    flat = jnp.concatenate([r_ref[x] for x in range(4)], axis=0)
+    right = widen([flat[:, 128 * j : 128 * j + 128] for j in range(4)])
+    marks = jnp.concatenate([class_ref[x] for x in range(4)], axis=0)
+    mark = [jnp.broadcast_to(marks[:, z : z + 1], (8, 128)) for z in range(8)]
+
+    diagonal = [jnp.zeros((8, 128), f32) for _ in range(8)]
+    totals = [jnp.zeros((8, 128), f32) for _ in range(8)]
+    shifts = [jnp.zeros((8, 128), f32) for _ in range(8)]
+    eye = iota((64, 128), 0) == (iota((64, 128), 1) & 63)
+    for k in range(16):
+        block = blocks_ref[k]
+        block = jnp.concatenate([block, block], axis=1)
+        diag_row = jnp.sum(jnp.where(eye, block, 0.0), axis=0, keepdims=True)
+        total_row = jnp.sum(block, axis=0, keepdims=True)
+        rest = jnp.where(eye, 0.0, block)
+        rest_hi = rest.astype(jnp.bfloat16)
+        w_hi[64 * k : 64 * k + 64, :] = rest_hi
+        w_lo[64 * k : 64 * k + 64, :] = (rest - rest_hi.astype(f32)).astype(jnp.bfloat16)
+        for z in range(8):
+            here = mark[z] == k
+            diagonal[z] = jnp.where(here, diag_row, diagonal[z])
+            totals[z] = jnp.where(here, total_row, totals[z])
+            shifts[z] = jnp.where(here, shift_ref[k], shifts[z])
+    inverse = [1.0 / d for d in diagonal]
+
+    wide_cell = iota((8, CELLS), 1)
+    wide_sub = iota((8, CELLS), 0)
+    own_cell = (gx * 2 + (wide_sub >> 2)) * 64 + gy * 16 + gz * 4
+
+    def cell_row(columns, scale):
+        row = jnp.zeros((8, CELLS), f32)
+        for j in range(4):
+            row = row + jnp.where(wide_cell == own_cell + j, columns[j], 0.0)
+        return scale * jnp.sum(row, axis=0, keepdims=True)
+
+    note_lane = iota((1, 128), 1)
+
+    def dots(*pairs):
+        row = jnp.zeros((1, 128), f32)
+        for at, (a, b) in enumerate(pairs):
+            acc = a[0] * b[0]
+            for z in range(1, 8):
+                acc = acc + a[z] * b[z]
+            acc = jnp.sum(jnp.sum(acc, axis=0, keepdims=True), axis=1, keepdims=True)
+            row = row + jnp.where(note_lane == at, 0.5 * acc, 0.0)
+        return row
+
+    def tell(at, message):
+        note_out[at] = message
+        note_in[at, me] = message
+        others(
+            lambda to: pltpu.make_async_remote_copy(
+                src_ref=note_out.at[at], dst_ref=note_in.at[at, me],
+                send_sem=note_send.at[at], recv_sem=note_recv.at[at],
+                device_id=to, device_id_type=MESH,
+            ).start()
+        )
+
+    def hear(at):
+        span = note_in.at[at, pl.ds(0, DEVICES - 1)]
+        pltpu.make_async_copy(span, span, note_recv.at[at]).wait()
+        return jnp.sum(note_in[at], axis=0)
+
+    def end_tell(at):
+        span = note_in.at[at, pl.ds(0, DEVICES - 1)]
+        pltpu.make_async_copy(span, span, note_send.at[at]).wait()
+
+    routes = (
+        (0, 1, gx < AXES[0] - 1, gx > 0, (gx + 1, gy, gz)),
+        (1, 1, gx > 0, gx < AXES[0] - 1, (gx - 1, gy, gz)),
+        (2, 2, gy < AXES[1] - 1, gy > 0, (gx, gy + 1, gz)),
+        (4, 2, gy > 0, gy < AXES[1] - 1, (gx, gy - 1, gz)),
+        (6, 1, gz < AXES[2] - 1, gz > 0, (gx, gy, gz + 1)),
+        (7, 1, gz > 0, gz < AXES[2] - 1, (gx, gy, gz - 1)),
+    )
+
+    def halo_copy(at, way):
+        tile, count, _, _, to = routes[way]
+        return pltpu.make_async_remote_copy(
+            src_ref=halo_out.at[at, pl.ds(tile, count)], dst_ref=halo_in.at[at, pl.ds(tile, count)],
+            send_sem=halo_send.at[at, way], recv_sem=halo_recv.at[at, way],
+            device_id=to, device_id_type=MESH,
+        )
+
+    odd = (sub & 1) == 1
+
+    def send_halo(at, u):
+        half = halves(u)
+        up, down = half[3], half[0]
+        up = jnp.where(sub >= 6, up, 0.0)
+        down = jnp.where(sub < 2, down, 0.0)
+        for m in range(3):
+            up = jnp.where((sub >> 1) == m, pltpu.roll(half[m], (2 * m + 2) % 8, 0), up)
+        for m in range(1, 4):
+            down = jnp.where((sub >> 1) == m, pltpu.roll(half[m], 2 * m, 0), down)
+        halo_out[at, 0] = up
+        halo_out[at, 1] = down
+        for j in range(2):
+            halo_out[at, 2 + j] = jnp.where(odd, half[2 * j], pltpu.roll(half[2 * j + 1], 7, 0))
+            halo_out[at, 4 + j] = jnp.where(odd, pltpu.roll(half[2 * j + 1], 1, 0), half[2 * j])
+        halo_out[at, 6] = u[7]
+        halo_out[at, 7] = u[0]
+        for way in range(6):
+            @pl.when(routes[way][2])
+            def _():
+                halo_copy(at, way).start()
+
+    def wait_halo(at):
+        for way in range(6):
+            @pl.when(routes[way][3])
+            def _():
+                halo_copy(at, way).wait_recv()
+
+    def end_halo(at):
+        for way in range(6):
+            @pl.when(routes[way][2])
+            def _():
+                halo_copy(at, way).wait_send()
+
+    def turn(tile, by):
+        return pltpu.roll(tile, by % 8, 0) if by % 8 else tile
+
+    def unpack_x(packed, row):
+        return widen([turn(packed, row - 2 * m) for m in range(4)])
+
+    def local_part(u):
+        top = jnp.concatenate(u, axis=0)
+        top_hi = top.astype(jnp.bfloat16).astype(f32)
+        top_lo = top - top_hi
+        classes = jnp.concatenate(mark, axis=0)
+        kind = classes - (iota((64, 128), 1) >> 6)
+        his, los = [], []
+        for p in range(8):
+            here = kind == 2 * p
+            his.append(jnp.where(here, top_hi, 0.0).astype(jnp.bfloat16))
+            los.append(jnp.where(here, top_lo, 0.0).astype(jnp.bfloat16))
+        hi, lo = jnp.concatenate(his, axis=1), jnp.concatenate(los, axis=1)
+        out = jnp.dot(hi, w_hi[...], preferred_element_type=f32)
+        out = out + jnp.dot(lo, w_hi[...], preferred_element_type=f32)
+        out = out + jnp.dot(hi, w_lo[...], preferred_element_type=f32)
+        return [out[8 * z : 8 * z + 8] + diagonal[z] * u[z] for z in range(8)]
+
+    def couple(u, at):
+        got = [halo_in[at, t] for t in range(8)]
+        x_before, x_after = unpack_x(got[0], 0), unpack_x(got[1], 6)
+        y_before = widen([pltpu.roll(got[2], 7, 0), got[2], pltpu.roll(got[3], 7, 0), got[3]])
+        y_after = widen([pltpu.roll(got[4], 1, 0), got[4], pltpu.roll(got[5], 1, 0), got[5]])
+        out = []
+        for z in range(8):
+            x_next = jnp.where(sub >= 6, x_after[z], pltpu.roll(u[z], 6, 0))
+            x_last = jnp.where(sub < 2, x_before[z], pltpu.roll(u[z], 2, 0))
+            y_next = jnp.where(odd, y_after[z], pltpu.roll(u[z], 7, 0))
+            y_last = jnp.where(odd, pltpu.roll(u[z], 1, 0), y_before[z])
+            z_next = u[z + 1] if z < 7 else got[7]
+            z_last = u[z - 1] if z > 0 else got[6]
+            acc = upper[0] * pltpu.roll(x_next, 48, 1) + lower[0] * pltpu.roll(x_last, 80, 1)
+            acc = acc + upper[1] * pltpu.roll(y_next, 12, 1) + lower[1] * pltpu.roll(y_last, 116, 1)
+            acc = acc + upper[2] * pltpu.roll(z_next, 3, 1) + lower[2] * pltpu.roll(z_last, 125, 1)
+            out.append(acc)
+        return out
+
+    def apply(u, at):
+        send_halo(at, u)
+        own = local_part(u)
+        wait_halo(at)
+        return [a - b for a, b in zip(own, couple(u, at))]
+
+    def tell_cells(at, left, extra):
+        sums = [jnp.sum(left[2 * j] + left[2 * j + 1], axis=1, keepdims=True) for j in range(4)]
+        tell(at, jnp.concatenate([cell_row(sums, 1.0 / 128.0), extra], axis=1))
+
+    def correct(q, iterate, left):
+        picked = jnp.sum(cells_ref[...] * q, axis=1, keepdims=True)
+        tiles = [jnp.broadcast_to(picked[8 * t : 8 * t + 8], (8, 128)) for t in range(22)]
+        own, x_up, x_down, y_up, y_down = tiles[:6], tiles[6:10], tiles[10:14], tiles[14:18], tiles[18:22]
+        out = []
+        for z in range(8):
+            j = z // 2
+            image = totals[z] * own[j + 1]
+            image = image - upper[0] * x_up[j] - lower[0] * x_down[j]
+            image = image - upper[1] * y_up[j] - lower[1] * y_down[j]
+            image = image - upper[2] * own[(z + 1) // 2 + 1] - lower[2] * own[(z - 1) // 2 + 1]
+            out.append(iterate[z] + own[j + 1] + 0.6 * (left[z] - image) * inverse[z])
+        return out
+
+    nothing = jnp.zeros((1, 128), f32)
+    first = [0.6 * a * b for a, b in zip(right, inverse)]
+    pl.semaphore_wait(barrier, DEVICES - 1)
+    columns = [(shifts[2 * j] + shifts[2 * j + 1])[:, :1] for j in range(4)]
+    tell(0, jnp.concatenate([cell_row(columns, 0.125), nothing], axis=1))
+    left = [a - b for a, b in zip(right, apply(first, 0))]
+    tell_cells(1, left, nothing)
+    shift_row = hear(0)[:, :CELLS]
+    cells_ref[...] = exact_dot(pick_cells(gx, gy, gz), coarse_matrix(shift_row))
+    z0 = correct(hear(1)[:, :CELLS], first, left)
+    w0 = apply(z0, 1)
+
+    start = [0.6 * a * b for a, b in zip(w0, inverse)]
+    left = [a - b for a, b in zip(w0, apply(start, 2))]
+    tell_cells(2, left, dots((right, z0), (z0, w0)))
+    heard = hear(2)
+    gamma, curve = heard[:, 256:257], heard[:, 257:258]
+    alpha = gamma / curve
+    u = correct(heard[:, :CELLS], start, left)
+    z1 = [a - alpha * b for a, b in zip(z0, u)]
+    w1 = apply(z1, 3)
+    r1 = [a - alpha * b for a, b in zip(right, w0)]
+    tell(3, jnp.concatenate([jnp.zeros((1, CELLS), f32), dots((r1, z1), (z1, w1), (z1, w0), (z0, w1))], axis=1))
+    heard = hear(3)
+    gamma_2 = heard[:, 256:257]
+    beta = gamma_2 / gamma
+    curve_2 = heard[:, 257:258] + beta * (heard[:, 258:259] + heard[:, 259:260]) + beta * beta * curve
+    alpha_2 = gamma_2 / curve_2
+    field = [alpha * a + alpha_2 * (b + beta * a) for a, b in zip(z0, z1)]
+    rest = [a - alpha_2 * (b + beta * c) for a, b, c in zip(r1, w1, w0)]
+    for ref, tiles in ((x_out, field), (r_out, rest)):
+        whole = jnp.concatenate(halves(tiles), axis=1)
+        for x in range(4):
+            ref[x] = whole[2 * x : 2 * x + 2, :]
+    for at in range(HALO_ROUNDS):
+        end_halo(at)
+        end_tell(at)
+
+
+def per_device_fused(right_side, element_class, class_blocks, class_shift, face_weights):
+    vmem, smem = pl.BlockSpec(memory_space=pltpu.VMEM), pl.BlockSpec(memory_space=pltpu.SMEM)
+    shape = jax.ShapeDtypeStruct(right_side.shape, f32)
+    return pl.pallas_call(
+        fused,
+        out_shape=(shape, shape),
+        in_specs=[vmem, vmem, vmem, smem, smem],
+        out_specs=(vmem, vmem),
+        scratch_shapes=[
+            pltpu.VMEM((HALO_ROUNDS, 8, 8, 128), f32),
+            pltpu.VMEM((HALO_ROUNDS, 8, 8, 128), f32),
+            pltpu.VMEM((HALO_ROUNDS, 1, MESSAGE), f32),
+            pltpu.VMEM((HALO_ROUNDS, DEVICES, 1, MESSAGE), f32),
+            pltpu.VMEM((1024, 128), jnp.bfloat16),
+            pltpu.VMEM((1024, 128), jnp.bfloat16),
+            pltpu.VMEM((176, CELLS), f32),
+            pltpu.SemaphoreType.DMA((HALO_ROUNDS, 6)),
+            pltpu.SemaphoreType.DMA((HALO_ROUNDS, 6)),
+            pltpu.SemaphoreType.DMA((HALO_ROUNDS,)),
+            pltpu.SemaphoreType.DMA((HALO_ROUNDS,)),
+        ],
+        compiler_params=pltpu.CompilerParams(
+            collective_id=0, has_side_effects=True, vmem_limit_bytes=32 * 1024 * 1024
+        ),
+    )(right_side, element_class, class_blocks, class_shift, face_weights)
+
+
 def solution(mesh):
     in_specs = (P("gx", "gy", "gz"), P("gx", "gy", "gz"), P(), P(), P())
     out_specs = (P("gx", "gy", "gz"), P("gx", "gy", "gz"))
+    small = tuple(mesh.shape[axis] for axis in ("gx", "gy", "gz")) == AXES
+    body = per_device_fused if small else per_device
     return jax.shard_map(
-        per_device, mesh=mesh, in_specs=in_specs, out_specs=out_specs, check_vma=False
-    )
+        body, mesh=mesh, in_specs=in_specs, out_specs=out_specs, check_vma=False
+    )

time: 324 us -> 40.7 us (0.13)
  blocking collectives: 123 us -> 0 us
  starting transfers between devices: 99.9 us -> 0 us
  waiting for transfers between devices: 57 us -> 0 us
  Pallas kernels: 0 us -> 34.8 us
  matrix products: 16.6 us -> 0 us
  other arithmetic: 11.1 us -> 0 us
  between operations: 5.99 us -> 0.65 us
  local copies, waits for them, and re-layouts: 9.31 us -> 4.96 us
    psum x3 -> x0, blocking collectives: 123 us -> none  [total(): return lax.psum(terms, ('gx', 'gy', 'gz'))]
    ppermute x46 -> x0, starting transfers between devices: 99.9 us -> none  [the longest x18 57.8 us: with_halo(): before = lax.ppermute(last, axis, up)]
    ppermute x46 -> x0, waiting for transfers between devices: 57 us -> none  [the longest x18 40.2 us: with_halo(): after = lax.ppermute(first, axis, down)]
    pallas_call x0 -> x1, Pallas kernels: none -> 34.8 us  [per_device_fused(): pl.pallas_call(fused, out_shape=(shape, shape), in_specs=[vmem, vmem, vme...]
    dot_general x20 -> x0, matrix products: 16.6 us -> none  [the longest x6 9.65 us: fine_apply(): jnp.dot(flat, wide_blocks, precision=highest)]
    reduce_sum x26 -> x0, other arithmetic: 3.66 us -> none  [the longest x23 1.78 us: coarsen(): values.reshape(size_x // 2, 2, size_y // 2, 2, size_z // 2, 2)]
    unnamed x11 -> x0, other arithmetic: 3.26 us -> none
  transfers between devices with their start and end apart: 46 -> 0, of which waited for: 22 -> 0; matrix products, arithmetic and copies ran while one was open for 7% -> 0% of each run, Pallas kernels for 0% -> 0%
where the time goes in v1:
time: 40.7 us; the launch traced here: 40.4 us
  Pallas kernels  34.8 us (86%)
  local copies, waits for them, and re-layouts  4.96 us (12%)
  between operations  0.65 us (2%)
    pallas_call x1, Pallas kernels, per_device_fused(): pl.pallas_call(fused, out_shape=(shape, shape), in_specs=[vmem, vmem, vme...  34.8 us
    unnamed x12, local copies, waits for them, and re-layouts  4.96 us

profile of v1, /device:TPU:0, one launch (start us, length us, event | category | flops | bytes accessed | tf_op | source)
XLA Modules:
  0.0 40.4 jit_solution(9872796937345084066)
XLA Ops:
  0.6 0.0 copy-start
  0.6 1.0 %copy-done = f32[16,64,64]{2,1,0:T(8,128)S(1)} copy-done((f32[16,64,64]{2,1,0:T(8,128)S(1)}, f32[16,64,64]{2,1,0:T(8,128)}, u32[]{:S(2)}) %copy-start) | copy-done | bytes 262168
  1.7 0.0 copy-start.1
  1.7 0.7 %copy-done.1 = f32[4,2,512]{2,1,0:T(2,128)S(1)} copy-done((f32[4,2,512]{2,1,0:T(2,128)S(1)}, f32[4,2,512]{2,1,0:T(2,128)}, u32[]{:S(2)}) %copy-start.1) | copy-done | bytes 16408
  2.4 0.0 copy-start.2
  2.4 0.7 %copy-done.2 = s32[4,2,8]{2,1,0:T(2,128)S(1)} copy-done((s32[4,2,8]{2,1,0:T(2,128)S(1)}, s32[4,2,8]{2,1,0:T(2,128)}, u32[]{:S(2)}) %copy-start.2) | copy-done | bytes 280
  3.1 0.0 copy-start.3
  3.1 0.7 %copy-done.3 = f32[16]{0:T(128)S(1)} copy-done((f32[16]{0:T(128)S(1)}, f32[16]{0:T(128)}, u32[]{:S(2)}) %copy-start.3) | copy-done | bytes 88
  3.7 0.0 copy-start.4
  3.7 0.7 %copy-done.4 = f32[3]{0:T(128)S(1)} copy-done((f32[3]{0:T(128)S(1)}, f32[3]{0:T(128)}, u32[]{:S(2)}) %copy-start.4) | copy-done | bytes 36
  4.4 34.8 %shard_map.68 = (f32[4,2,512]{2,1,0:T(2,128)S(1)}, f32[4,2,512]{2,1,0:T(2,128)S(1)}) custom-call(f32[4,2,512]{2,1,0:T(2,128)S(1)} %copy-done.1, s32[4,2,8]{2,1,0:T(2,128)S(1)} %copy-done.2, f32[16,64,64]{2,1,0:T(8,128)S(1)} %copy-done, f32[16]{0:T(128)S(1)} %copy-done.3, f32[3]{0:T(128)S(1)} %copy-done.4), custom_call_target="tpu_custom_call" | custom-call | tf_op jit(solution)/shard_map/pallas_call | solution.py:548
  39.2 0.6 %copy.9 = f32[4,2,512]{2,1,0:T(2,128)} copy(f32[4,2,512]{2,1,0:T(2,128)S(1)} %get-tuple-element.4) | data formatting | bytes 32768
  39.8 0.6 %copy.10 = f32[4,2,512]{2,1,0:T(2,128)} copy(f32[4,2,512]{2,1,0:T(2,128)S(1)} %get-tuple-element.5) | data formatting | bytes 32768
Async XLA Ops:
  0.6 1.0 %copy-start = (f32[16,64,64]{2,1,0:T(8,128)S(1)}, f32[16,64,64]{2,1,0:T(8,128)}, u32[]{:S(2)}) copy-start(f32[16,64,64]{2,1,0:T(8,128)} %blocks_ref.1) | copy-start | bytes 786436
  1.7 0.7 %copy-start.1 = (f32[4,2,512]{2,1,0:T(2,128)S(1)}, f32[4,2,512]{2,1,0:T(2,128)}, u32[]{:S(2)}) copy-start(f32[4,2,512]{2,1,0:T(2,128)} %r_ref.1) | copy-start | bytes 49156
  2.4 0.7 %copy-start.2 = (s32[4,2,8]{2,1,0:T(2,128)S(1)}, s32[4,2,8]{2,1,0:T(2,128)}, u32[]{:S(2)}) copy-start(s32[4,2,8]{2,1,0:T(2,128)} %class_ref.1) | copy-start | bytes 772
  3.1 0.7 %copy-start.3 = (f32[16]{0:T(128)S(1)}, f32[16]{0:T(128)}, u32[]{:S(2)}) copy-start(f32[16]{0:T(128)} %shift_ref.1) | copy-start | bytes 196
  3.7 0.7 %copy-start.4 = (f32[3]{0:T(128)S(1)}, f32[3]{0:T(128)}, u32[]{:S(2)}) copy-start(f32[3]{0:T(128)} %weight_ref.1) | copy-start | bytes 40

commit v2 on v1

--- a/solution.py
+++ b/solution.py
@@ -215,7 +215,14 @@
 
 
 def exact_dot(a, b):
-    return jnp.dot(a, b, precision=highest, preferred_element_type=f32)
+    a = a.astype(jnp.bfloat16)
+    total_dot = None
+    for _ in range(3):
+        part = b.astype(jnp.bfloat16)
+        b = b - part.astype(f32)
+        term = jnp.dot(a, part, preferred_element_type=f32)
+        total_dot = term if total_dot is None else total_dot + term
+    return total_dot
 
 
 def neighbours(count, bits_y, bits_z, section_y, section_z):
@@ -269,22 +276,38 @@
 def pick_cells(gx, gy, gz):
     rows = []
     s, cell = iota((8, CELLS), 0), iota((8, CELLS), 1)
+    cx, cy, cz = cell >> 6, cell >> 4 & 3, cell & 15
+
+    def pick(x, y, z):
+        hit = (cx == ((gx * 4 + x) >> 1)) & (cy == ((gy * 2 + y) >> 1)) & (cz == gz * 4 + z)
+        rows.append(jnp.where(hit, 1.0, 0.0).astype(f32))
+
     x, y = s >> 1, s & 1
-    cx, cy, cz = cell >> 6, cell >> 4 & 3, cell & 15
     for dx, dy, zs in ((0, 0, range(-1, 5)), (1, 0, range(4)), (-1, 0, range(4)), (0, 1, range(4)), (0, -1, range(4))):
-        at_x = (gx * 4 + x + dx) >> 1
-        at_y = (gy * 2 + y + dy) >> 1
         for z in zs:
-            hit = (cx == at_x) & (cy == at_y) & (cz == gz * 4 + z)
-            rows.append(jnp.where(hit, 1.0, 0.0).astype(f32))
+            pick(x + dx, y + dy, z)
+    pairs = ((-1, y, s >> 1), (4, y, s >> 1))
+    pairs += ((x, -1, 1 - y), (x, -1, 3 - y), (x, 2, y), (x, 2, y + 2), (x, y, -1), (x, y, 4))
+    for gone_x, gone_y, gone_z in pairs:
+        pick(gone_x, gone_y, gone_z)
+        for dx, dy, dz in ((1, 0, 0), (-1, 0, 0), (0, 1, 0), (0, -1, 0), (0, 0, 1), (0, 0, -1)):
+            pick(gone_x + dx, gone_y + dy, gone_z + dz)
     return jnp.concatenate(rows, axis=0)
 
 
 def fused(
-    r_ref, class_ref, blocks_ref, shift_ref, weight_ref, x_out, r_out,
+    r_hbm, class_hbm, blocks_hbm, shift_hbm, weight_hbm, x_out, r_out,
+    r_ref, class_ref, blocks_ref, shift_ref, weight_ref,
     halo_out, halo_in, note_out, note_in, w_hi, w_lo, cells_ref,
-    halo_send, halo_recv, note_send, note_recv,
+    load_sem, halo_send, halo_recv, note_send, note_recv,
 ):
+    loads = (
+        (blocks_hbm, blocks_ref), (r_hbm, r_ref), (class_hbm, class_ref),
+        (shift_hbm, shift_ref), (weight_hbm, weight_ref),
+    )
+    loads = [pltpu.make_async_copy(a, b, load_sem.at[i]) for i, (a, b) in enumerate(loads)]
+    for load in loads:
+        load.start()
     gx, gy, gz = lax.axis_index("gx"), lax.axis_index("gy"), lax.axis_index("gz")
     me = gx * 16 + gy * 4 + gz
 
@@ -299,6 +322,9 @@
     barrier = pltpu.get_barrier_semaphore()
     halo_in[...] = jnp.zeros_like(halo_in)
     others(lambda to: pl.semaphore_signal(barrier, inc=1, device_id=to, device_id_type=MESH))
+
+    for load in loads:
+        load.wait()
 
     lane = iota((8, 128), 1)
     sub = iota((8, 128), 0)
@@ -396,34 +422,39 @@
 
     def halo_copy(at, way):
         tile, count, _, _, to = routes[way]
+        span = pl.ds(3 * tile, 3 * count if at == 0 else count)
         return pltpu.make_async_remote_copy(
-            src_ref=halo_out.at[at, pl.ds(tile, count)], dst_ref=halo_in.at[at, pl.ds(tile, count)],
+            src_ref=halo_out.at[at, span], dst_ref=halo_in.at[at, span],
             send_sem=halo_send.at[at, way], recv_sem=halo_recv.at[at, way],
             device_id=to, device_id_type=MESH,
         )
 
     odd = (sub & 1) == 1
 
-    def send_halo(at, u):
-        half = halves(u)
-        up, down = half[3], half[0]
-        up = jnp.where(sub >= 6, up, 0.0)
-        down = jnp.where(sub < 2, down, 0.0)
-        for m in range(3):
-            up = jnp.where((sub >> 1) == m, pltpu.roll(half[m], (2 * m + 2) % 8, 0), up)
-        for m in range(1, 4):
-            down = jnp.where((sub >> 1) == m, pltpu.roll(half[m], 2 * m, 0), down)
-        halo_out[at, 0] = up
-        halo_out[at, 1] = down
-        for j in range(2):
-            halo_out[at, 2 + j] = jnp.where(odd, half[2 * j], pltpu.roll(half[2 * j + 1], 7, 0))
-            halo_out[at, 4 + j] = jnp.where(odd, pltpu.roll(half[2 * j + 1], 1, 0), half[2 * j])
-        halo_out[at, 6] = u[7]
-        halo_out[at, 7] = u[0]
+    places = [(0, 1, 0), (1, 1, 0), (2, 2, 0), (2, 2, 1), (4, 2, 0), (4, 2, 1), (6, 1, 0), (7, 1, 0)]
+
+    def send_halo(at, *fields):
+        for f, u in enumerate(fields):
+            half = halves(u)
+            up = jnp.where(sub >= 6, half[3], 0.0)
+            down = jnp.where(sub < 2, half[0], 0.0)
+            for m in range(3):
+                up = jnp.where((sub >> 1) == m, pltpu.roll(half[m], (2 * m + 2) % 8, 0), up)
+            for m in range(1, 4):
+                down = jnp.where((sub >> 1) == m, pltpu.roll(half[m], 2 * m, 0), down)
+            tiles = [up, down]
+            tiles += [jnp.where(odd, half[2 * j], pltpu.roll(half[2 * j + 1], 7, 0)) for j in range(2)]
+            tiles += [jnp.where(odd, pltpu.roll(half[2 * j + 1], 1, 0), half[2 * j]) for j in range(2)]
+            tiles += [u[7], u[0]]
+            for (tile, count, j), value in zip(places, tiles):
+                halo_out[at, 3 * tile + f * count + j] = value
         for way in range(6):
             @pl.when(routes[way][2])
             def _():
                 halo_copy(at, way).start()
+
+    def ghosts(at, f=0):
+        return [halo_in[at, 3 * tile + f * count + j] for tile, count, j in places]
 
     def wait_halo(at):
         for way in range(6):
@@ -460,8 +491,7 @@
         out = out + jnp.dot(hi, w_lo[...], preferred_element_type=f32)
         return [out[8 * z : 8 * z + 8] + diagonal[z] * u[z] for z in range(8)]
 
-    def couple(u, at):
-        got = [halo_in[at, t] for t in range(8)]
+    def couple(u, got):
         x_before, x_after = unpack_x(got[0], 0), unpack_x(got[1], 6)
         y_before = widen([pltpu.roll(got[2], 7, 0), got[2], pltpu.roll(got[3], 7, 0), got[3]])
         y_after = widen([pltpu.roll(got[4], 1, 0), got[4], pltpu.roll(got[5], 1, 0), got[5]])
@@ -479,51 +509,69 @@
             out.append(acc)
         return out
 
-    def apply(u, at):
-        send_halo(at, u)
-        own = local_part(u)
-        wait_halo(at)
-        return [a - b for a, b in zip(own, couple(u, at))]
+    def minus(a, b):
+        return [p - q for p, q in zip(a, b)]
 
     def tell_cells(at, left, extra):
         sums = [jnp.sum(left[2 * j] + left[2 * j + 1], axis=1, keepdims=True) for j in range(4)]
         tell(at, jnp.concatenate([cell_row(sums, 1.0 / 128.0), extra], axis=1))
 
-    def correct(q, iterate, left):
+    def correct(q, source, iterate, left, at):
         picked = jnp.sum(cells_ref[...] * q, axis=1, keepdims=True)
-        tiles = [jnp.broadcast_to(picked[8 * t : 8 * t + 8], (8, 128)) for t in range(22)]
+        tiles = [jnp.broadcast_to(picked[8 * t : 8 * t + 8], (8, 128)) for t in range(78)]
         own, x_up, x_down, y_up, y_down = tiles[:6], tiles[6:10], tiles[10:14], tiles[14:18], tiles[18:22]
-        out = []
+        rest, scaled = [], []
         for z in range(8):
             j = z // 2
             image = totals[z] * own[j + 1]
             image = image - upper[0] * x_up[j] - lower[0] * x_down[j]
             image = image - upper[1] * y_up[j] - lower[1] * y_down[j]
             image = image - upper[2] * own[(z + 1) // 2 + 1] - lower[2] * own[(z - 1) // 2 + 1]
-            out.append(iterate[z] + own[j + 1] + 0.6 * (left[z] - image) * inverse[z])
-        return out
+            rest.append(left[z] - image)
+            scaled.append(rest[z] * inverse[z])
+        own_part = local_part(scaled)
+        wait_halo(at)
+        got = []
+        for g, (sent, inv, tot) in enumerate(zip(ghosts(at), ghosts(0, 1), ghosts(0, 2))):
+            mid, xu, xd, yu, yd, zu, zd = tiles[22 + 7 * g : 29 + 7 * g]
+            if g < 6:
+                zu, zd = jnp.where(low, mid, zu), jnp.where(low, zd, mid)
+            pull = upper[0] * xu + lower[0] * xd + upper[1] * yu + lower[1] * yd
+            pull = pull + upper[2] * zu + lower[2] * zd
+            got.append(sent - tot * mid + inv * pull)
+        near = couple(scaled, got)
+        result = [iterate[z] + own[z // 2 + 1] + 0.6 * scaled[z] for z in range(8)]
+        image = [source[z] - rest[z] + 0.6 * (own_part[z] - near[z]) for z in range(8)]
+        return result, image
+
+    def descend(source, at, *fields):
+        iterate = [0.6 * a * b for a, b in zip(source, inverse)]
+        send_halo(at, iterate, *fields)
+        own_part = local_part(iterate)
+        wait_halo(at)
+        left = minus(source, minus(own_part, couple(iterate, ghosts(at))))
+        send_halo(at + 1, [a * b for a, b in zip(left, inverse)])
+        return iterate, left
 
     nothing = jnp.zeros((1, 128), f32)
-    first = [0.6 * a * b for a, b in zip(right, inverse)]
     pl.semaphore_wait(barrier, DEVICES - 1)
     columns = [(shifts[2 * j] + shifts[2 * j + 1])[:, :1] for j in range(4)]
     tell(0, jnp.concatenate([cell_row(columns, 0.125), nothing], axis=1))
-    left = [a - b for a, b in zip(right, apply(first, 0))]
+    ratio = [a * b for a, b in zip(totals, inverse)]
+    first, left = descend(right, 0, inverse, ratio)
     tell_cells(1, left, nothing)
     shift_row = hear(0)[:, :CELLS]
     cells_ref[...] = exact_dot(pick_cells(gx, gy, gz), coarse_matrix(shift_row))
-    z0 = correct(hear(1)[:, :CELLS], first, left)
-    w0 = apply(z0, 1)
-
-    start = [0.6 * a * b for a, b in zip(w0, inverse)]
-    left = [a - b for a, b in zip(w0, apply(start, 2))]
+    z0, w0 = correct(hear(1)[:, :CELLS], right, first, left, 1)
+
+    start, left = descend(w0, 2)
     tell_cells(2, left, dots((right, z0), (z0, w0)))
     heard = hear(2)
     gamma, curve = heard[:, 256:257], heard[:, 257:258]
     alpha = gamma / curve
-    u = correct(heard[:, :CELLS], start, left)
+    u, v = correct(heard[:, :CELLS], w0, start, left, 3)
     z1 = [a - alpha * b for a, b in zip(z0, u)]
-    w1 = apply(z1, 3)
+    w1 = [a - alpha * b for a, b in zip(w0, v)]
     r1 = [a - alpha * b for a, b in zip(right, w0)]
     tell(3, jnp.concatenate([jnp.zeros((1, CELLS), f32), dots((r1, z1), (z1, w1), (z1, w0), (z0, w1))], axis=1))
     heard = hear(3)
@@ -543,21 +591,27 @@
 
 
 def per_device_fused(right_side, element_class, class_blocks, class_shift, face_weights):
-    vmem, smem = pl.BlockSpec(memory_space=pltpu.VMEM), pl.BlockSpec(memory_space=pltpu.SMEM)
+    vmem, hbm = pl.BlockSpec(memory_space=pltpu.VMEM), pl.BlockSpec(memory_space=pltpu.HBM)
     shape = jax.ShapeDtypeStruct(right_side.shape, f32)
     return pl.pallas_call(
         fused,
         out_shape=(shape, shape),
-        in_specs=[vmem, vmem, vmem, smem, smem],
+        in_specs=[hbm] * 5,
         out_specs=(vmem, vmem),
         scratch_shapes=[
-            pltpu.VMEM((HALO_ROUNDS, 8, 8, 128), f32),
-            pltpu.VMEM((HALO_ROUNDS, 8, 8, 128), f32),
+            pltpu.VMEM(right_side.shape, f32),
+            pltpu.VMEM(element_class.shape, jnp.int32),
+            pltpu.VMEM(class_blocks.shape, f32),
+            pltpu.SMEM(class_shift.shape, f32),
+            pltpu.SMEM(face_weights.shape, f32),
+            pltpu.VMEM((HALO_ROUNDS, 24, 8, 128), f32),
+            pltpu.VMEM((HALO_ROUNDS, 24, 8, 128), f32),
             pltpu.VMEM((HALO_ROUNDS, 1, MESSAGE), f32),
             pltpu.VMEM((HALO_ROUNDS, DEVICES, 1, MESSAGE), f32),
             pltpu.VMEM((1024, 128), jnp.bfloat16),
             pltpu.VMEM((1024, 128), jnp.bfloat16),
-            pltpu.VMEM((176, CELLS), f32),
+            pltpu.VMEM((624, CELLS), f32),
+            pltpu.SemaphoreType.DMA((5,)),
             pltpu.SemaphoreType.DMA((HALO_ROUNDS, 6)),
             pltpu.SemaphoreType.DMA((HALO_ROUNDS, 6)),
             pltpu.SemaphoreType.DMA((HALO_ROUNDS,)),

time: 40.7 us -> 35.3 us (0.87)
  Pallas kernels: 34.8 us -> 29.4 us
    pallas_call x1, Pallas kernels: 34.8 us -> 29.4 us  [per_device_fused(): pl.pallas_call(fused, out_shape=(shape, shape), in_specs=[hbm] * 5, out_s...]
where the time goes in v2:
time: 35.3 us; the launch traced here: 35 us
  Pallas kernels  29.4 us (83%)
  local copies, waits for them, and re-layouts  4.96 us (14%)
  between operations  0.65 us (2%)
    pallas_call x1, Pallas kernels, per_device_fused(): pl.pallas_call(fused, out_shape=(shape, shape), in_specs=[hbm] * 5, out_s...  29.4 us
    unnamed x12, local copies, waits for them, and re-layouts  4.96 us

profile of v2, /device:TPU:0, one launch (start us, length us, event | category | flops | bytes accessed | tf_op | source)
XLA Modules:
  0.0 35.0 jit_solution(417395667500667706)
XLA Ops:
  0.6 0.0 copy-start
  0.6 1.0 %copy-done = f32[16,64,64]{2,1,0:T(8,128)S(1)} copy-done((f32[16,64,64]{2,1,0:T(8,128)S(1)}, f32[16,64,64]{2,1,0:T(8,128)}, u32[]{:S(2)}) %copy-start) | copy-done | bytes 262168
  1.7 0.0 copy-start.1
  1.7 0.7 %copy-done.1 = f32[4,2,512]{2,1,0:T(2,128)S(1)} copy-done((f32[4,2,512]{2,1,0:T(2,128)S(1)}, f32[4,2,512]{2,1,0:T(2,128)}, u32[]{:S(2)}) %copy-start.1) | copy-done | bytes 16408
  2.4 0.0 copy-start.2
  2.4 0.7 %copy-done.2 = s32[4,2,8]{2,1,0:T(2,128)S(1)} copy-done((s32[4,2,8]{2,1,0:T(2,128)S(1)}, s32[4,2,8]{2,1,0:T(2,128)}, u32[]{:S(2)}) %copy-start.2) | copy-done | bytes 280
  3.1 0.0 copy-start.3
  3.1 0.7 %copy-done.3 = f32[16]{0:T(128)S(1)} copy-done((f32[16]{0:T(128)S(1)}, f32[16]{0:T(128)}, u32[]{:S(2)}) %copy-start.3) | copy-done | bytes 88
  3.7 0.0 copy-start.4
  3.7 0.7 %copy-done.4 = f32[3]{0:T(128)S(1)} copy-done((f32[3]{0:T(128)S(1)}, f32[3]{0:T(128)}, u32[]{:S(2)}) %copy-start.4) | copy-done | bytes 36
  4.4 29.4 %shard_map.68 = (f32[4,2,512]{2,1,0:T(2,128)S(1)}, f32[4,2,512]{2,1,0:T(2,128)S(1)}) custom-call(f32[4,2,512]{2,1,0:T(2,128)S(1)} %copy-done.1, s32[4,2,8]{2,1,0:T(2,128)S(1)} %copy-done.2, f32[16,64,64]{2,1,0:T(8,128)S(1)} %copy-done, f32[16]{0:T(128)S(1)} %copy-done.3, f32[3]{0:T(128)S(1)} %copy-done.4), custom_call_target="tpu_custom_call" | custom-call | tf_op jit(solution)/shard_map/pallas_call | solution.py:596
  33.8 0.6 %copy.9 = f32[4,2,512]{2,1,0:T(2,128)} copy(f32[4,2,512]{2,1,0:T(2,128)S(1)} %get-tuple-element.4) | data formatting | bytes 32768
  34.4 0.6 %copy.10 = f32[4,2,512]{2,1,0:T(2,128)} copy(f32[4,2,512]{2,1,0:T(2,128)S(1)} %get-tuple-element.5) | data formatting | bytes 32768
Async XLA Ops:
  0.6 1.0 %copy-start = (f32[16,64,64]{2,1,0:T(8,128)S(1)}, f32[16,64,64]{2,1,0:T(8,128)}, u32[]{:S(2)}) copy-start(f32[16,64,64]{2,1,0:T(8,128)} %blocks_hbm.1) | copy-start | bytes 786436
  1.7 0.7 %copy-start.1 = (f32[4,2,512]{2,1,0:T(2,128)S(1)}, f32[4,2,512]{2,1,0:T(2,128)}, u32[]{:S(2)}) copy-start(f32[4,2,512]{2,1,0:T(2,128)} %r_hbm.1) | copy-start | bytes 49156
  2.4 0.7 %copy-start.2 = (s32[4,2,8]{2,1,0:T(2,128)S(1)}, s32[4,2,8]{2,1,0:T(2,128)}, u32[]{:S(2)}) copy-start(s32[4,2,8]{2,1,0:T(2,128)} %class_hbm.1) | copy-start | bytes 772
  3.1 0.7 %copy-start.3 = (f32[16]{0:T(128)S(1)}, f32[16]{0:T(128)}, u32[]{:S(2)}) copy-start(f32[16]{0:T(128)} %shift_hbm.1) | copy-start | bytes 196
  3.7 0.7 %copy-start.4 = (f32[3]{0:T(128)S(1)}, f32[3]{0:T(128)}, u32[]{:S(2)}) copy-start(f32[3]{0:T(128)} %weight_hbm.1) | copy-start | bytes 40

commit v3 on v2

--- a/solution.py
+++ b/solution.py
@@ -202,7 +202,6 @@
 
 
 AXES = (2, 4, 4)
-DEVICES = 32
 CELLS = 256
 MESSAGE = 384
 HALO_ROUNDS = 4
@@ -237,10 +236,9 @@
     return jnp.where((apart == 1) & same, 1.0, 0.0).astype(f32)
 
 
-def coarse_matrix(shift_row):
+def coarse_matrix(shift_row, beside_1):
     i, j = iota((CELLS, CELLS), 0), iota((CELLS, CELLS), 1)
     eye = jnp.where(i == j, 1.0, 0.0).astype(f32)
-    beside_1 = neighbours(CELLS, 2, 4, 1, 3)
     beside_2 = neighbours(32, 1, 3, 1, 3)
     j2, cell = iota((32, CELLS), 0), iota((32, CELLS), 1)
     parent = (cell >> 7) * 16 + (cell >> 5 & 1) * 8 + (cell >> 1 & 7)
@@ -258,7 +256,7 @@
     d3 = 6.0 + 0.015625 * jnp.sum(
         jnp.where((cellw >> 2 & 3) == j3w, shift_row, 0.0), axis=1, keepdims=True
     )
-    q2 = 0.25 * exact_dot(down_1, 0.4 * eye + 0.6 * beside_1 / d1_row)
+    q2 = 0.25 * exact_dot(down_1, 0.4 * eye + 0.6 * beside_1.astype(f32) / d1_row)
     x2 = 0.6 * q2 / d2
     q3 = 0.25 * exact_dot(down_2, 0.4 * q2 + exact_dot(beside_2, x2))
     x3 = 0.6 * q3 / d3
@@ -298,7 +296,7 @@
 def fused(
     r_hbm, class_hbm, blocks_hbm, shift_hbm, weight_hbm, x_out, r_out,
     r_ref, class_ref, blocks_ref, shift_ref, weight_ref,
-    halo_out, halo_in, note_out, note_in, w_hi, w_lo, cells_ref,
+    halo_out, halo_in, note_out, note_in, w_hi, w_lo, cells_ref, pick_ref, beside_ref,
     load_sem, halo_send, halo_recv, note_send, note_recv,
 ):
     loads = (
@@ -309,19 +307,18 @@
     for load in loads:
         load.start()
     gx, gy, gz = lax.axis_index("gx"), lax.axis_index("gy"), lax.axis_index("gz")
-    me = gx * 16 + gy * 4 + gz
-
-    def others(act):
-        def step(k, carry):
-            to = lax.rem(me + k, DEVICES)
-            act((to // 16, lax.rem(to // 4, 4), lax.rem(to, 4)))
-            return carry
-
-        lax.fori_loop(1, DEVICES, step, 0)
+
+    plane = gx * 4 + gy
+    along = [(gx, gy, lax.rem(gz + k, 4)) for k in range(1, 4)]
+    across = [lax.rem(plane + k, 8) for k in range(1, 8)]
+    across = [(to // 4, lax.rem(to, 4), gz) for to in across]
 
     barrier = pltpu.get_barrier_semaphore()
     halo_in[...] = jnp.zeros_like(halo_in)
-    others(lambda to: pl.semaphore_signal(barrier, inc=1, device_id=to, device_id_type=MESH))
+    for to in along + across:
+        pl.semaphore_signal(barrier, inc=1, device_id=to, device_id_type=MESH)
+    pick_ref[...] = pick_cells(gx, gy, gz).astype(jnp.bfloat16)
+    beside_ref[...] = neighbours(CELLS, 2, 4, 1, 3).astype(jnp.bfloat16)
 
     for load in loads:
         load.wait()
@@ -391,25 +388,30 @@
             row = row + jnp.where(note_lane == at, 0.5 * acc, 0.0)
         return row
 
-    def tell(at, message):
-        note_out[at] = message
-        note_in[at, me] = message
-        others(
-            lambda to: pltpu.make_async_remote_copy(
-                src_ref=note_out.at[at], dst_ref=note_in.at[at, me],
-                send_sem=note_send.at[at], recv_sem=note_recv.at[at],
+    def tell(at, step, message):
+        base, me, partners = ((0, gz, along), (4, plane, across))[step]
+        note_out[at, step] = message
+        note_in[at, base + me] = message
+        for to in partners:
+            pltpu.make_async_remote_copy(
+                src_ref=note_out.at[at, step], dst_ref=note_in.at[at, base + me],
+                send_sem=note_send.at[at, step], recv_sem=note_recv.at[at, step],
                 device_id=to, device_id_type=MESH,
             ).start()
-        )
-
-    def hear(at):
-        span = note_in.at[at, pl.ds(0, DEVICES - 1)]
-        pltpu.make_async_copy(span, span, note_recv.at[at]).wait()
-        return jnp.sum(note_in[at], axis=0)
+
+    def hear(at, step):
+        base, count = ((0, 4), (4, 8))[step]
+        span = note_in.at[at, pl.ds(base, count - 1)]
+        pltpu.make_async_copy(span, span, note_recv.at[at, step]).wait()
+        return jnp.sum(note_in[at, base : base + count], axis=0)
+
+    def relay(at):
+        tell(at, 1, hear(at, 0))
 
     def end_tell(at):
-        span = note_in.at[at, pl.ds(0, DEVICES - 1)]
-        pltpu.make_async_copy(span, span, note_send.at[at]).wait()
+        for step, count in ((0, 3), (1, 7)):
+            span = note_in.at[at, pl.ds(0, count)]
+            pltpu.make_async_copy(span, span, note_send.at[at, step]).wait()
 
     routes = (
         (0, 1, gx < AXES[0] - 1, gx > 0, (gx + 1, gy, gz)),
@@ -514,7 +516,7 @@
 
     def tell_cells(at, left, extra):
         sums = [jnp.sum(left[2 * j] + left[2 * j + 1], axis=1, keepdims=True) for j in range(4)]
-        tell(at, jnp.concatenate([cell_row(sums, 1.0 / 128.0), extra], axis=1))
+        tell(at, 0, jnp.concatenate([cell_row(sums, 1.0 / 128.0), extra], axis=1))
 
     def correct(q, source, iterate, left, at):
         picked = jnp.sum(cells_ref[...] * q, axis=1, keepdims=True)
@@ -544,9 +546,11 @@
         image = [source[z] - rest[z] + 0.6 * (own_part[z] - near[z]) for z in range(8)]
         return result, image
 
-    def descend(source, at, *fields):
+    def descend(source, at, *fields, between=None):
         iterate = [0.6 * a * b for a, b in zip(source, inverse)]
         send_halo(at, iterate, *fields)
+        if between is not None:
+            between()
         own_part = local_part(iterate)
         wait_halo(at)
         left = minus(source, minus(own_part, couple(iterate, ghosts(at))))
@@ -554,27 +558,31 @@
         return iterate, left
 
     nothing = jnp.zeros((1, 128), f32)
-    pl.semaphore_wait(barrier, DEVICES - 1)
+    pl.semaphore_wait(barrier, 10)
     columns = [(shifts[2 * j] + shifts[2 * j + 1])[:, :1] for j in range(4)]
-    tell(0, jnp.concatenate([cell_row(columns, 0.125), nothing], axis=1))
     ratio = [a * b for a, b in zip(totals, inverse)]
-    first, left = descend(right, 0, inverse, ratio)
+    shift_message = jnp.concatenate([cell_row(columns, 0.125), nothing], axis=1)
+    first, left = descend(right, 0, inverse, ratio, between=lambda: tell(0, 0, shift_message))
+    relay(0)
     tell_cells(1, left, nothing)
-    shift_row = hear(0)[:, :CELLS]
-    cells_ref[...] = exact_dot(pick_cells(gx, gy, gz), coarse_matrix(shift_row))
-    z0, w0 = correct(hear(1)[:, :CELLS], right, first, left, 1)
+    coarse = coarse_matrix(hear(0, 1)[:, :CELLS], beside_ref[...])
+    relay(1)
+    cells_ref[...] = exact_dot(pick_ref[...], coarse)
+    z0, w0 = correct(hear(1, 1)[:, :CELLS], right, first, left, 1)
 
     start, left = descend(w0, 2)
     tell_cells(2, left, dots((right, z0), (z0, w0)))
-    heard = hear(2)
+    relay(2)
+    heard = hear(2, 1)
     gamma, curve = heard[:, 256:257], heard[:, 257:258]
     alpha = gamma / curve
     u, v = correct(heard[:, :CELLS], w0, start, left, 3)
     z1 = [a - alpha * b for a, b in zip(z0, u)]
     w1 = [a - alpha * b for a, b in zip(w0, v)]
     r1 = [a - alpha * b for a, b in zip(right, w0)]
-    tell(3, jnp.concatenate([jnp.zeros((1, CELLS), f32), dots((r1, z1), (z1, w1), (z1, w0), (z0, w1))], axis=1))
-    heard = hear(3)
+    tell(3, 0, jnp.concatenate([jnp.zeros((1, CELLS), f32), dots((r1, z1), (z1, w1), (z1, w0), (z0, w1))], axis=1))
+    relay(3)
+    heard = hear(3, 1)
     gamma_2 = heard[:, 256:257]
     beta = gamma_2 / gamma
     curve_2 = heard[:, 257:258] + beta * (heard[:, 258:259] + heard[:, 259:260]) + beta * beta * curve
@@ -606,19 +614,21 @@
             pltpu.SMEM(face_weights.shape, f32),
             pltpu.VMEM((HALO_ROUNDS, 24, 8, 128), f32),
             pltpu.VMEM((HALO_ROUNDS, 24, 8, 128), f32),
-            pltpu.VMEM((HALO_ROUNDS, 1, MESSAGE), f32),
-            pltpu.VMEM((HALO_ROUNDS, DEVICES, 1, MESSAGE), f32),
+            pltpu.VMEM((HALO_ROUNDS, 2, 1, MESSAGE), f32),
+            pltpu.VMEM((HALO_ROUNDS, 12, 1, MESSAGE), f32),
             pltpu.VMEM((1024, 128), jnp.bfloat16),
             pltpu.VMEM((1024, 128), jnp.bfloat16),
             pltpu.VMEM((624, CELLS), f32),
+            pltpu.VMEM((624, CELLS), jnp.bfloat16),
+            pltpu.VMEM((CELLS, CELLS), jnp.bfloat16),
             pltpu.SemaphoreType.DMA((5,)),
             pltpu.SemaphoreType.DMA((HALO_ROUNDS, 6)),
             pltpu.SemaphoreType.DMA((HALO_ROUNDS, 6)),
-            pltpu.SemaphoreType.DMA((HALO_ROUNDS,)),
-            pltpu.SemaphoreType.DMA((HALO_ROUNDS,)),
+            pltpu.SemaphoreType.DMA((HALO_ROUNDS, 2)),
+            pltpu.SemaphoreType.DMA((HALO_ROUNDS, 2)),
         ],
         compiler_params=pltpu.CompilerParams(
-            collective_id=0, has_side_effects=True, vmem_limit_bytes=32 * 1024 * 1024
+            collective_id=0, has_side_effects=True
         ),
     )(right_side, element_class, class_blocks, class_shift, face_weights)
 

time: 35.3 us -> 40.2 us (1.14)
  Pallas kernels: 29.4 us -> 37.4 us
  local copies, waits for them, and re-layouts: 4.96 us -> 1.94 us
    pallas_call x1, Pallas kernels: 29.4 us -> 37.4 us  [per_device_fused(): pl.pallas_call(fused, out_shape=(shape, shape), in_specs=[hbm] * 5, out_s...]
    unnamed x12 -> x4, local copies, waits for them, and re-layouts: 4.96 us -> 1.94 us
where the time goes in v3:
time: 40.2 us; the launch traced here: 40 us
  Pallas kernels  37.4 us (93%)
  local copies, waits for them, and re-layouts  1.94 us (5%)
  between operations  0.65 us (2%)
    pallas_call x1, Pallas kernels, per_device_fused(): pl.pallas_call(fused, out_shape=(shape, shape), in_specs=[hbm] * 5, out_s...  37.4 us
    unnamed x4, local copies, waits for them, and re-layouts  1.94 us

profile of v3, /device:TPU:0, one launch (start us, length us, event | category | flops | bytes accessed | tf_op | source)
XLA Modules:
  0.0 40.0 jit_solution(11965308891313036903)
XLA Ops:
  0.6 37.4 %shard_map.68 = (f32[4,2,512]{2,1,0:T(2,128)}, f32[4,2,512]{2,1,0:T(2,128)}) custom-call(f32[4,2,512]{2,1,0:T(2,128)} %r_hbm.1, s32[4,2,8]{2,1,0:T(2,128)} %class_hbm.1, f32[16,64,64]{2,1,0:T(8,128)} %blocks_hbm.1, f32[16]{0:T(128)} %shift_hbm.1, f32[3]{0:T(128)} %weight_hbm.1), custom_call_target="tpu_custom_call" | custom-call | tf_op jit(solution)/shard_map/pallas_call | solution.py:604
  38.1 0.0 copy-start
  38.1 1.3 %copy.9 = f32[4,2,512]{2,1,0:T(2,128)} copy(f32[4,2,512]{2,1,0:T(2,128)} %get-tuple-element.4) | data formatting | bytes 32768
  39.4 0.0 copy-done
  39.4 0.6 %copy.10 = f32[4,2,512]{2,1,0:T(2,128)} copy(f32[4,2,512]{2,1,0:T(2,128)S(1)} %copy-done) | data formatting | bytes 32768
Async XLA Ops:
  38.1 1.3 %copy-start = (f32[4,2,512]{2,1,0:T(2,128)S(1)}, f32[4,2,512]{2,1,0:T(2,128)}, u32[]{:S(2)}) copy-start(f32[4,2,512]{2,1,0:T(2,128)} %get-tuple-element.5) | copy-start | bytes 49156

commit v4 on v2

--- a/solution.py
+++ b/solution.py
@@ -202,9 +202,9 @@
 
 
 AXES = (2, 4, 4)
+CELLS = 256
 DEVICES = 32
-CELLS = 256
-MESSAGE = 384
+MESSAGE = 256
 HALO_ROUNDS = 4
 MESH = pl.DeviceIdType.MESH
 f32 = jnp.float32
@@ -237,10 +237,9 @@
     return jnp.where((apart == 1) & same, 1.0, 0.0).astype(f32)
 
 
-def coarse_matrix(shift_row):
+def coarse_matrix(shift_row, beside_1):
     i, j = iota((CELLS, CELLS), 0), iota((CELLS, CELLS), 1)
     eye = jnp.where(i == j, 1.0, 0.0).astype(f32)
-    beside_1 = neighbours(CELLS, 2, 4, 1, 3)
     beside_2 = neighbours(32, 1, 3, 1, 3)
     j2, cell = iota((32, CELLS), 0), iota((32, CELLS), 1)
     parent = (cell >> 7) * 16 + (cell >> 5 & 1) * 8 + (cell >> 1 & 7)
@@ -258,7 +257,7 @@
     d3 = 6.0 + 0.015625 * jnp.sum(
         jnp.where((cellw >> 2 & 3) == j3w, shift_row, 0.0), axis=1, keepdims=True
     )
-    q2 = 0.25 * exact_dot(down_1, 0.4 * eye + 0.6 * beside_1 / d1_row)
+    q2 = 0.25 * exact_dot(down_1, 0.4 * eye + 0.6 * beside_1.astype(f32) / d1_row)
     x2 = 0.6 * q2 / d2
     q3 = 0.25 * exact_dot(down_2, 0.4 * q2 + exact_dot(beside_2, x2))
     x3 = 0.6 * q3 / d3
@@ -298,7 +297,7 @@
 def fused(
     r_hbm, class_hbm, blocks_hbm, shift_hbm, weight_hbm, x_out, r_out,
     r_ref, class_ref, blocks_ref, shift_ref, weight_ref,
-    halo_out, halo_in, note_out, note_in, w_hi, w_lo, cells_ref,
+    halo_out, halo_in, note_out, note_in, w_ref, cells_ref, pick_ref, beside_ref,
     load_sem, halo_send, halo_recv, note_send, note_recv,
 ):
     loads = (
@@ -309,19 +308,17 @@
     for load in loads:
         load.start()
     gx, gy, gz = lax.axis_index("gx"), lax.axis_index("gy"), lax.axis_index("gz")
+
     me = gx * 16 + gy * 4 + gz
-
-    def others(act):
-        def step(k, carry):
-            to = lax.rem(me + k, DEVICES)
-            act((to // 16, lax.rem(to // 4, 4), lax.rem(to, 4)))
-            return carry
-
-        lax.fori_loop(1, DEVICES, step, 0)
-
+    ring_y = [gy] + [lax.rem(gy + k, 4) for k in range(1, 4)]
+    ring_z = [gz] + [lax.rem(gz + k, 4) for k in range(1, 4)]
+    others = [(x, y, z) for y in ring_y for x in (gx, 1 - gx) for z in ring_z][:0:-1]
     barrier = pltpu.get_barrier_semaphore()
     halo_in[...] = jnp.zeros_like(halo_in)
-    others(lambda to: pl.semaphore_signal(barrier, inc=1, device_id=to, device_id_type=MESH))
+    for to in others:
+        pl.semaphore_signal(barrier, inc=1, device_id=to, device_id_type=MESH)
+    pick_ref[...] = pick_cells(gx, gy, gz).astype(jnp.bfloat16)
+    beside_ref[...] = neighbours(CELLS, 2, 4, 1, 3).astype(jnp.bfloat16)
 
     for load in loads:
         load.wait()
@@ -352,16 +349,17 @@
     diagonal = [jnp.zeros((8, 128), f32) for _ in range(8)]
     totals = [jnp.zeros((8, 128), f32) for _ in range(8)]
     shifts = [jnp.zeros((8, 128), f32) for _ in range(8)]
-    eye = iota((64, 128), 0) == (iota((64, 128), 1) & 63)
+    eye = iota((64, 64), 0) == iota((64, 64), 1)
     for k in range(16):
         block = blocks_ref[k]
-        block = jnp.concatenate([block, block], axis=1)
-        diag_row = jnp.sum(jnp.where(eye, block, 0.0), axis=0, keepdims=True)
-        total_row = jnp.sum(block, axis=0, keepdims=True)
         rest = jnp.where(eye, 0.0, block)
-        rest_hi = rest.astype(jnp.bfloat16)
-        w_hi[64 * k : 64 * k + 64, :] = rest_hi
-        w_lo[64 * k : 64 * k + 64, :] = (rest - rest_hi.astype(f32)).astype(jnp.bfloat16)
+        rest_hi = rest.astype(jnp.bfloat16).astype(f32)
+        both = jnp.concatenate([rest_hi, rest - rest_hi], axis=1)
+        w_ref[64 * k : 64 * k + 64, :] = both.astype(jnp.bfloat16)
+        rest_row = jnp.sum(rest, axis=0, keepdims=True)
+        diag_row = jnp.sum(block - rest, axis=0, keepdims=True)
+        diag_row = jnp.concatenate([diag_row, diag_row], axis=1)
+        total_row = jnp.concatenate([rest_row, rest_row], axis=1) + diag_row
         for z in range(8):
             here = mark[z] == k
             diagonal[z] = jnp.where(here, diag_row, diagonal[z])
@@ -369,14 +367,12 @@
             shifts[z] = jnp.where(here, shift_ref[k], shifts[z])
     inverse = [1.0 / d for d in diagonal]
 
-    wide_cell = iota((8, CELLS), 1)
-    wide_sub = iota((8, CELLS), 0)
-    own_cell = (gx * 2 + (wide_sub >> 2)) * 64 + gy * 16 + gz * 4
+    own_cell = (sub >> 2) * 64 + gy * 16 + gz * 4
 
     def cell_row(columns, scale):
-        row = jnp.zeros((8, CELLS), f32)
+        row = jnp.zeros((8, 128), f32)
         for j in range(4):
-            row = row + jnp.where(wide_cell == own_cell + j, columns[j], 0.0)
+            row = row + jnp.where(lane == own_cell + j, columns[j], 0.0)
         return scale * jnp.sum(row, axis=0, keepdims=True)
 
     note_lane = iota((1, 128), 1)
@@ -391,24 +387,30 @@
             row = row + jnp.where(note_lane == at, 0.5 * acc, 0.0)
         return row
 
+    widths = (128, 128, 256, 128)
+
+    def note(ref, at, slot):
+        return ref.at[at, slot, :, pl.ds(0, widths[at])]
+
     def tell(at, message):
-        note_out[at] = message
-        note_in[at, me] = message
-        others(
-            lambda to: pltpu.make_async_remote_copy(
-                src_ref=note_out.at[at], dst_ref=note_in.at[at, me],
+        note_out[at, :, : widths[at]] = message
+        note_in[at, me, :, : widths[at]] = message
+        for to in others:
+            pltpu.make_async_remote_copy(
+                src_ref=note_out.at[at, :, pl.ds(0, widths[at])], dst_ref=note(note_in, at, me),
                 send_sem=note_send.at[at], recv_sem=note_recv.at[at],
                 device_id=to, device_id_type=MESH,
             ).start()
-        )
 
     def hear(at):
-        span = note_in.at[at, pl.ds(0, DEVICES - 1)]
+        span = note(note_in, at, pl.ds(0, DEVICES - 1))
         pltpu.make_async_copy(span, span, note_recv.at[at]).wait()
-        return jnp.sum(note_in[at], axis=0)
+        cells = note_in[at, :, :, :128]
+        cells = [jnp.sum(cells[:16], axis=0), jnp.sum(cells[16:], axis=0)]
+        return jnp.concatenate(cells, axis=1)
 
     def end_tell(at):
-        span = note_in.at[at, pl.ds(0, DEVICES - 1)]
+        span = note(note_in, at, pl.ds(0, DEVICES - 1))
         pltpu.make_async_copy(span, span, note_send.at[at]).wait()
 
     routes = (
@@ -478,17 +480,13 @@
         top = jnp.concatenate(u, axis=0)
         top_hi = top.astype(jnp.bfloat16).astype(f32)
         top_lo = top - top_hi
-        classes = jnp.concatenate(mark, axis=0)
-        kind = classes - (iota((64, 128), 1) >> 6)
-        his, los = [], []
-        for p in range(8):
-            here = kind == 2 * p
-            his.append(jnp.where(here, top_hi, 0.0).astype(jnp.bfloat16))
-            los.append(jnp.where(here, top_lo, 0.0).astype(jnp.bfloat16))
-        hi, lo = jnp.concatenate(his, axis=1), jnp.concatenate(los, axis=1)
-        out = jnp.dot(hi, w_hi[...], preferred_element_type=f32)
-        out = out + jnp.dot(lo, w_hi[...], preferred_element_type=f32)
-        out = out + jnp.dot(hi, w_lo[...], preferred_element_type=f32)
+        top = jnp.concatenate([top_hi, top_lo], axis=0)
+        classes = jnp.concatenate(mark + mark, axis=0)
+        kind = classes - (iota((128, 128), 1) >> 6)
+        parts = [jnp.where(kind == 2 * p, top, 0.0).astype(jnp.bfloat16) for p in range(8)]
+        out = jnp.dot(jnp.concatenate(parts, axis=1), w_ref[...], preferred_element_type=f32)
+        out = out[:64] + out[64:]
+        out = out + pltpu.roll(out, 64, 1)
         return [out[8 * z : 8 * z + 8] + diagonal[z] * u[z] for z in range(8)]
 
     def couple(u, got):
@@ -512,9 +510,9 @@
     def minus(a, b):
         return [p - q for p, q in zip(a, b)]
 
-    def tell_cells(at, left, extra):
+    def tell_cells(at, left, *extra):
         sums = [jnp.sum(left[2 * j] + left[2 * j + 1], axis=1, keepdims=True) for j in range(4)]
-        tell(at, jnp.concatenate([cell_row(sums, 1.0 / 128.0), extra], axis=1))
+        tell(at, jnp.concatenate([cell_row(sums, 1.0 / 128.0), *extra], axis=1))
 
     def correct(q, source, iterate, left, at):
         picked = jnp.sum(cells_ref[...] * q, axis=1, keepdims=True)
@@ -544,40 +542,43 @@
         image = [source[z] - rest[z] + 0.6 * (own_part[z] - near[z]) for z in range(8)]
         return result, image
 
-    def descend(source, at, *fields):
+    def descend(source, at, *fields, between=None):
         iterate = [0.6 * a * b for a, b in zip(source, inverse)]
         send_halo(at, iterate, *fields)
+        if between is not None:
+            between()
         own_part = local_part(iterate)
         wait_halo(at)
         left = minus(source, minus(own_part, couple(iterate, ghosts(at))))
         send_halo(at + 1, [a * b for a, b in zip(left, inverse)])
         return iterate, left
 
-    nothing = jnp.zeros((1, 128), f32)
     pl.semaphore_wait(barrier, DEVICES - 1)
     columns = [(shifts[2 * j] + shifts[2 * j + 1])[:, :1] for j in range(4)]
-    tell(0, jnp.concatenate([cell_row(columns, 0.125), nothing], axis=1))
     ratio = [a * b for a, b in zip(totals, inverse)]
-    first, left = descend(right, 0, inverse, ratio)
-    tell_cells(1, left, nothing)
-    shift_row = hear(0)[:, :CELLS]
-    cells_ref[...] = exact_dot(pick_cells(gx, gy, gz), coarse_matrix(shift_row))
-    z0, w0 = correct(hear(1)[:, :CELLS], right, first, left, 1)
+    shift_message = cell_row(columns, 0.125)
+    first, left = descend(right, 0, inverse, ratio, between=lambda: tell(0, shift_message))
+    tell_cells(1, left)
+    coarse = coarse_matrix(hear(0), beside_ref[...])
+    cells_ref[...] = exact_dot(pick_ref[...], coarse)
+    z0, w0 = correct(hear(1), right, first, left, 1)
 
     start, left = descend(w0, 2)
     tell_cells(2, left, dots((right, z0), (z0, w0)))
     heard = hear(2)
-    gamma, curve = heard[:, 256:257], heard[:, 257:258]
+    heard_dots = jnp.sum(note_in[2, :, :, 128:], axis=0)
+    gamma, curve = heard_dots[:, 0:1], heard_dots[:, 1:2]
     alpha = gamma / curve
-    u, v = correct(heard[:, :CELLS], w0, start, left, 3)
+    u, v = correct(heard, w0, start, left, 3)
     z1 = [a - alpha * b for a, b in zip(z0, u)]
     w1 = [a - alpha * b for a, b in zip(w0, v)]
     r1 = [a - alpha * b for a, b in zip(right, w0)]
-    tell(3, jnp.concatenate([jnp.zeros((1, CELLS), f32), dots((r1, z1), (z1, w1), (z1, w0), (z0, w1))], axis=1))
+    tell(3, dots((r1, z1), (z1, w1), (z1, w0), (z0, w1)))
     heard = hear(3)
-    gamma_2 = heard[:, 256:257]
+    heard = heard[:, :128] + heard[:, 128:]
+    gamma_2 = heard[:, 0:1]
     beta = gamma_2 / gamma
-    curve_2 = heard[:, 257:258] + beta * (heard[:, 258:259] + heard[:, 259:260]) + beta * beta * curve
+    curve_2 = heard[:, 1:2] + beta * (heard[:, 2:3] + heard[:, 3:4]) + beta * beta * curve
     alpha_2 = gamma_2 / curve_2
     field = [alpha * a + alpha_2 * (b + beta * a) for a, b in zip(z0, z1)]
     rest = [a - alpha_2 * (b + beta * c) for a, b, c in zip(r1, w1, w0)]
@@ -609,8 +610,9 @@
             pltpu.VMEM((HALO_ROUNDS, 1, MESSAGE), f32),
             pltpu.VMEM((HALO_ROUNDS, DEVICES, 1, MESSAGE), f32),
             pltpu.VMEM((1024, 128), jnp.bfloat16),
-            pltpu.VMEM((1024, 128), jnp.bfloat16),
             pltpu.VMEM((624, CELLS), f32),
+            pltpu.VMEM((624, CELLS), jnp.bfloat16),
+            pltpu.VMEM((CELLS, CELLS), jnp.bfloat16),
             pltpu.SemaphoreType.DMA((5,)),
             pltpu.SemaphoreType.DMA((HALO_ROUNDS, 6)),
             pltpu.SemaphoreType.DMA((HALO_ROUNDS, 6)),
@@ -618,7 +620,7 @@
             pltpu.SemaphoreType.DMA((HALO_ROUNDS,)),
         ],
         compiler_params=pltpu.CompilerParams(
-            collective_id=0, has_side_effects=True, vmem_limit_bytes=32 * 1024 * 1024
+            collective_id=0, has_side_effects=True
         ),
     )(right_side, element_class, class_blocks, class_shift, face_weights)
 

time: 35.3 us -> 30.8 us (0.87)
  local copies, waits for them, and re-layouts: 4.96 us -> 1.94 us
  Pallas kernels: 29.4 us -> 28 us
    unnamed x12 -> x4, local copies, waits for them, and re-layouts: 4.96 us -> 1.94 us
    pallas_call x1, Pallas kernels: 29.4 us -> 28 us  [per_device_fused(): pl.pallas_call(fused, out_shape=(shape, shape), in_specs=[hbm] * 5, out_s...]
where the time goes in v4:
time: 30.8 us; the launch traced here: 30.6 us
  Pallas kernels  28 us (91%)
  local copies, waits for them, and re-layouts  1.94 us (6%)
  between operations  0.65 us (2%)
    pallas_call x1, Pallas kernels, per_device_fused(): pl.pallas_call(fused, out_shape=(shape, shape), in_specs=[hbm] * 5, out_s...  28 us
    unnamed x4, local copies, waits for them, and re-layouts  1.94 us

profile of v4, /device:TPU:0, one launch (start us, length us, event | category | flops | bytes accessed | tf_op | source)
XLA Modules:
  0.0 30.6 jit_solution(18285122989868500532)
XLA Ops:
  0.6 28.0 %shard_map.68 = (f32[4,2,512]{2,1,0:T(2,128)}, f32[4,2,512]{2,1,0:T(2,128)}) custom-call(f32[4,2,512]{2,1,0:T(2,128)} %r_hbm.1, s32[4,2,8]{2,1,0:T(2,128)} %class_hbm.1, f32[16,64,64]{2,1,0:T(8,128)} %blocks_hbm.1, f32[16]{0:T(128)} %shift_hbm.1, f32[3]{0:T(128)} %weight_hbm.1), custom_call_target="tpu_custom_call" | custom-call | tf_op jit(solution)/shard_map/pallas_call | solution.py:597
  28.7 0.0 copy-start
  28.7 1.3 %copy.9 = f32[4,2,512]{2,1,0:T(2,128)} copy(f32[4,2,512]{2,1,0:T(2,128)} %get-tuple-element.4) | data formatting | bytes 32768
  30.0 0.0 copy-done
  30.0 0.6 %copy.10 = f32[4,2,512]{2,1,0:T(2,128)} copy(f32[4,2,512]{2,1,0:T(2,128)S(1)} %copy-done) | data formatting | bytes 32768
Async XLA Ops:
  28.7 1.3 %copy-start = (f32[4,2,512]{2,1,0:T(2,128)S(1)}, f32[4,2,512]{2,1,0:T(2,128)}, u32[]{:S(2)}) copy-start(f32[4,2,512]{2,1,0:T(2,128)} %get-tuple-element.5) | copy-start | bytes 49156

commit v5 on v4

--- a/solution.py
+++ b/solution.py
@@ -295,7 +295,7 @@
 
 
 def fused(
-    r_hbm, class_hbm, blocks_hbm, shift_hbm, weight_hbm, x_out, r_out,
+    r_hbm, class_hbm, blocks_hbm, shift_hbm, weight_hbm, out_ref,
     r_ref, class_ref, blocks_ref, shift_ref, weight_ref,
     halo_out, halo_in, note_out, note_in, w_ref, cells_ref, pick_ref, beside_ref,
     load_sem, halo_send, halo_recv, note_send, note_recv,
@@ -346,26 +346,31 @@
     marks = jnp.concatenate([class_ref[x] for x in range(4)], axis=0)
     mark = [jnp.broadcast_to(marks[:, z : z + 1], (8, 128)) for z in range(8)]
 
-    diagonal = [jnp.zeros((8, 128), f32) for _ in range(8)]
-    totals = [jnp.zeros((8, 128), f32) for _ in range(8)]
-    shifts = [jnp.zeros((8, 128), f32) for _ in range(8)]
+    def by_class(rows):
+        out = [jnp.broadcast_to(rows[0], (8, 128)) for _ in range(8)]
+        for k in range(1, 16):
+            out = [jnp.where(here == k, rows[k], old) for here, old in zip(mark, out)]
+        return out
+
+    def twice(row):
+        return jnp.concatenate([row, row], axis=1)
+
     eye = iota((64, 64), 0) == iota((64, 64), 1)
-    for k in range(16):
-        block = blocks_ref[k]
-        rest = jnp.where(eye, 0.0, block)
-        rest_hi = rest.astype(jnp.bfloat16).astype(f32)
-        both = jnp.concatenate([rest_hi, rest - rest_hi], axis=1)
-        w_ref[64 * k : 64 * k + 64, :] = both.astype(jnp.bfloat16)
-        rest_row = jnp.sum(rest, axis=0, keepdims=True)
-        diag_row = jnp.sum(block - rest, axis=0, keepdims=True)
-        diag_row = jnp.concatenate([diag_row, diag_row], axis=1)
-        total_row = jnp.concatenate([rest_row, rest_row], axis=1) + diag_row
-        for z in range(8):
-            here = mark[z] == k
-            diagonal[z] = jnp.where(here, diag_row, diagonal[z])
-            totals[z] = jnp.where(here, total_row, totals[z])
-            shifts[z] = jnp.where(here, shift_ref[k], shifts[z])
+    diag_rows = [
+        twice(jnp.sum(jnp.where(eye, blocks_ref[k], 0.0), axis=0, keepdims=True)) for k in range(16)
+    ]
+    diagonal = by_class(diag_rows)
     inverse = [1.0 / d for d in diagonal]
+
+    def prepare():
+        rows = []
+        for k in range(16):
+            rest = jnp.where(eye, 0.0, blocks_ref[k])
+            rest_hi = rest.astype(jnp.bfloat16).astype(f32)
+            both = jnp.concatenate([rest_hi, rest - rest_hi], axis=1)
+            w_ref[64 * k : 64 * k + 64, :] = both.astype(jnp.bfloat16)
+            rows.append(twice(jnp.sum(rest, axis=0, keepdims=True)) + diag_rows[k])
+        return by_class(rows), by_class([shift_ref[k] for k in range(16)])
 
     own_cell = (sub >> 2) * 64 + gy * 16 + gz * 4
 
@@ -424,7 +429,7 @@
 
     def halo_copy(at, way):
         tile, count, _, _, to = routes[way]
-        span = pl.ds(3 * tile, 3 * count if at == 0 else count)
+        span = pl.ds(3 * tile, 3 * count if at == 1 else count)
         return pltpu.make_async_remote_copy(
             src_ref=halo_out.at[at, span], dst_ref=halo_in.at[at, span],
             send_sem=halo_send.at[at, way], recv_sem=halo_recv.at[at, way],
@@ -510,11 +515,11 @@
     def minus(a, b):
         return [p - q for p, q in zip(a, b)]
 
-    def tell_cells(at, left, *extra):
+    def cell_sums(left):
         sums = [jnp.sum(left[2 * j] + left[2 * j + 1], axis=1, keepdims=True) for j in range(4)]
-        tell(at, jnp.concatenate([cell_row(sums, 1.0 / 128.0), *extra], axis=1))
-
-    def correct(q, source, iterate, left, at):
+        return cell_row(sums, 1.0 / 128.0)
+
+    def correct(q, source, iterate, left, totals, at):
         picked = jnp.sum(cells_ref[...] * q, axis=1, keepdims=True)
         tiles = [jnp.broadcast_to(picked[8 * t : 8 * t + 8], (8, 128)) for t in range(78)]
         own, x_up, x_down, y_up, y_down = tiles[:6], tiles[6:10], tiles[10:14], tiles[14:18], tiles[18:22]
@@ -530,7 +535,7 @@
         own_part = local_part(scaled)
         wait_halo(at)
         got = []
-        for g, (sent, inv, tot) in enumerate(zip(ghosts(at), ghosts(0, 1), ghosts(0, 2))):
+        for g, (sent, inv, tot) in enumerate(zip(ghosts(at), ghosts(1, 1), ghosts(1, 2))):
             mid, xu, xd, yu, yd, zu, zd = tiles[22 + 7 * g : 29 + 7 * g]
             if g < 6:
                 zu, zd = jnp.where(low, mid, zu), jnp.where(low, zd, mid)
@@ -542,38 +547,46 @@
         image = [source[z] - rest[z] + 0.6 * (own_part[z] - near[z]) for z in range(8)]
         return result, image
 
-    def descend(source, at, *fields, between=None):
-        iterate = [0.6 * a * b for a, b in zip(source, inverse)]
-        send_halo(at, iterate, *fields)
-        if between is not None:
-            between()
+    def scale(a, b):
+        return [p * q for p, q in zip(a, b)]
+
+    def remainder(source, iterate, at):
         own_part = local_part(iterate)
         wait_halo(at)
-        left = minus(source, minus(own_part, couple(iterate, ghosts(at))))
-        send_halo(at + 1, [a * b for a, b in zip(left, inverse)])
-        return iterate, left
-
+        return minus(source, minus(own_part, couple(iterate, ghosts(at))))
+
+    first = [0.6 * a for a in scale(right, inverse)]
     pl.semaphore_wait(barrier, DEVICES - 1)
+    send_halo(0, first)
+    totals, shifts = prepare()
     columns = [(shifts[2 * j] + shifts[2 * j + 1])[:, :1] for j in range(4)]
-    ratio = [a * b for a, b in zip(totals, inverse)]
-    shift_message = cell_row(columns, 0.125)
-    first, left = descend(right, 0, inverse, ratio, between=lambda: tell(0, shift_message))
-    tell_cells(1, left)
+    tell(0, cell_row(columns, 0.125))
+    left = remainder(right, first, 0)
+    tell(1, cell_sums(left))
+    send_halo(1, scale(left, inverse), inverse, scale(totals, inverse))
     coarse = coarse_matrix(hear(0), beside_ref[...])
     cells_ref[...] = exact_dot(pick_ref[...], coarse)
-    z0, w0 = correct(hear(1), right, first, left, 1)
-
-    start, left = descend(w0, 2)
-    tell_cells(2, left, dots((right, z0), (z0, w0)))
+    z0, w0 = correct(hear(1), right, first, left, totals, 1)
+
+    start = [0.6 * a for a in scale(w0, inverse)]
+    send_halo(2, start)
+    early_dots = dots((right, z0), (z0, w0))
+    left = remainder(w0, start, 2)
+    tell(2, jnp.concatenate([cell_sums(left), early_dots], axis=1))
+    send_halo(3, scale(left, inverse))
     heard = hear(2)
     heard_dots = jnp.sum(note_in[2, :, :, 128:], axis=0)
     gamma, curve = heard_dots[:, 0:1], heard_dots[:, 1:2]
     alpha = gamma / curve
-    u, v = correct(heard, w0, start, left, 3)
+    u, v = correct(heard, w0, start, left, totals, 3)
     z1 = [a - alpha * b for a, b in zip(z0, u)]
     w1 = [a - alpha * b for a, b in zip(w0, v)]
     r1 = [a - alpha * b for a, b in zip(right, w0)]
     tell(3, dots((r1, z1), (z1, w1), (z1, w0), (z0, w1)))
+    for at in range(HALO_ROUNDS):
+        end_halo(at)
+    for at in range(3):
+        end_tell(at)
     heard = hear(3)
     heard = heard[:, :128] + heard[:, 128:]
     gamma_2 = heard[:, 0:1]
@@ -582,23 +595,20 @@
     alpha_2 = gamma_2 / curve_2
     field = [alpha * a + alpha_2 * (b + beta * a) for a, b in zip(z0, z1)]
     rest = [a - alpha_2 * (b + beta * c) for a, b, c in zip(r1, w1, w0)]
-    for ref, tiles in ((x_out, field), (r_out, rest)):
-        whole = jnp.concatenate(halves(tiles), axis=1)
-        for x in range(4):
-            ref[x] = whole[2 * x : 2 * x + 2, :]
-    for at in range(HALO_ROUNDS):
-        end_halo(at)
-        end_tell(at)
+    whole = jnp.concatenate(halves(field) + halves(rest), axis=1)
+    for x in range(4):
+        out_ref[x] = whole[2 * x : 2 * x + 2, :]
+    end_tell(3)
 
 
 def per_device_fused(right_side, element_class, class_blocks, class_shift, face_weights):
     vmem, hbm = pl.BlockSpec(memory_space=pltpu.VMEM), pl.BlockSpec(memory_space=pltpu.HBM)
-    shape = jax.ShapeDtypeStruct(right_side.shape, f32)
-    return pl.pallas_call(
+    size_x, size_y, width = right_side.shape
+    both = pl.pallas_call(
         fused,
-        out_shape=(shape, shape),
+        out_shape=jax.ShapeDtypeStruct((size_x, size_y, 2 * width), f32),
         in_specs=[hbm] * 5,
-        out_specs=(vmem, vmem),
+        out_specs=vmem,
         scratch_shapes=[
             pltpu.VMEM(right_side.shape, f32),
             pltpu.VMEM(element_class.shape, jnp.int32),
@@ -623,6 +633,7 @@
             collective_id=0, has_side_effects=True
         ),
     )(right_side, element_class, class_blocks, class_shift, face_weights)
+    return both[:, :, :width], both[:, :, width:]
 
 
 def solution(mesh):

time: 30.8 us -> 30.1 us (0.977)
  local copies, waits for them, and re-layouts: 1.94 us -> 1.35 us
    unnamed x4 -> x0, local copies, waits for them, and re-layouts: 1.94 us -> none
    slice x0 -> x1, local copies, waits for them, and re-layouts: none -> 1.35 us  [per_device_fused(): return (both[:, :, :width], both[:, :, width:])]
where the time goes in v5:
time: 30.1 us; the launch traced here: 29.9 us
  Pallas kernels  27.9 us (93%)
  local copies, waits for them, and re-layouts  1.35 us (4%)
  between operations  0.64 us (2%)
    pallas_call x1, Pallas kernels, per_device_fused(): pl.pallas_call(fused, out_shape=jax.ShapeDtypeStruct((size_x, size_y, 2 *...  27.9 us
    slice x1, local copies, waits for them, and re-layouts, per_device_fused(): return (both[:, :, :width], both[:, :, width:])  1.35 us

profile of v5, /device:TPU:0, one launch (start us, length us, event | category | flops | bytes accessed | tf_op | source)
XLA Modules:
  0.0 29.9 jit_solution(1080360407936960960)
XLA Ops:
  0.6 27.9 %shard_map.68 = f32[4,2,1024]{2,1,0:T(2,128)} custom-call(f32[4,2,512]{2,1,0:T(2,128)} %r_hbm.1, s32[4,2,8]{2,1,0:T(2,128)} %class_hbm.1, f32[16,64,64]{2,1,0:T(8,128)} %blocks_hbm.1, f32[16]{0:T(128)} %shift_hbm.1, f32[3]{0:T(128)} %weight_hbm.1), custom_call_target="tpu_custom_call" | custom-call | tf_op jit(solution)/shard_map/pallas_call | solution.py:607
  28.5 1.3 %fusion = (f32[4,2,512]{2,1,0:T(2,128)}, f32[4,2,512]{2,1,0:T(2,128)}) fusion(f32[4,2,1024]{2,1,0:T(2,128)} %shard_map.68), kind=kLoop, calls=%fused_computation | loop fusion | bytes 65536 | tf_op jit(solution)/shard_map/slice | solution.py:636

commit v6 on v5

--- a/solution.py
+++ b/solution.py
@@ -204,7 +204,8 @@
 AXES = (2, 4, 4)
 CELLS = 256
 DEVICES = 32
-MESSAGE = 256
+MESSAGE = 384
+NOTE_ROUNDS = 3
 HALO_ROUNDS = 4
 MESH = pl.DeviceIdType.MESH
 f32 = jnp.float32
@@ -214,10 +215,10 @@
     return lax.broadcasted_iota(jnp.int32, shape, dim)
 
 
-def exact_dot(a, b):
+def exact_dot(a, b, parts=2):
     a = a.astype(jnp.bfloat16)
     total_dot = None
-    for _ in range(3):
+    for _ in range(parts):
         part = b.astype(jnp.bfloat16)
         b = b - part.astype(f32)
         term = jnp.dot(a, part, preferred_element_type=f32)
@@ -297,7 +298,7 @@
 def fused(
     r_hbm, class_hbm, blocks_hbm, shift_hbm, weight_hbm, out_ref,
     r_ref, class_ref, blocks_ref, shift_ref, weight_ref,
-    halo_out, halo_in, note_out, note_in, w_ref, cells_ref, pick_ref, beside_ref,
+    halo_out, halo_in, note_out, note_in, w_ref, cells_ref, coarse_ref, pick_ref, beside_ref,
     load_sem, halo_send, halo_recv, note_send, note_recv,
 ):
     loads = (
@@ -392,7 +393,7 @@
             row = row + jnp.where(note_lane == at, 0.5 * acc, 0.0)
         return row
 
-    widths = (128, 128, 256, 128)
+    widths = (384, 384, 128)
 
     def note(ref, at, slot):
         return ref.at[at, slot, :, pl.ds(0, widths[at])]
@@ -410,9 +411,7 @@
     def hear(at):
         span = note(note_in, at, pl.ds(0, DEVICES - 1))
         pltpu.make_async_copy(span, span, note_recv.at[at]).wait()
-        cells = note_in[at, :, :, :128]
-        cells = [jnp.sum(cells[:16], axis=0), jnp.sum(cells[16:], axis=0)]
-        return jnp.concatenate(cells, axis=1)
+        return note_in[at, :, :, : widths[at]]
 
     def end_tell(at):
         span = note(note_in, at, pl.ds(0, DEVICES - 1))
@@ -515,12 +514,32 @@
     def minus(a, b):
         return [p - q for p, q in zip(a, b)]
 
-    def cell_sums(left):
-        sums = [jnp.sum(left[2 * j] + left[2 * j + 1], axis=1, keepdims=True) for j in range(4)]
-        return cell_row(sums, 1.0 / 128.0)
-
-    def correct(q, source, iterate, left, totals, at):
-        picked = jnp.sum(cells_ref[...] * q, axis=1, keepdims=True)
+    def cell_message(w, v, totals):
+        cell, s = iota((8, CELLS), 1), iota((8, CELLS), 0)
+
+        def offset(dx, dy):
+            x, y = (gx * 4 + (s >> 1) + dx) >> 1, (gy * 2 + (s & 1) + dy) >> 1
+            inside = (x >= 0) & (x < 4) & (y >= 0) & (y < 4)
+            return jnp.where(inside, cell - (x * 64 + y * 16 + gz * 4), 4096)
+
+        def place(values, off, z):
+            return jnp.where(off == z, jnp.sum(values, axis=1, keepdims=True), 0.0)
+
+        pair = [0.6 * (v[2 * j] + v[2 * j + 1]) for j in range(4)]
+        here = offset(0, 0)
+        row = place(0.6 * lower[2] * v[0], here, jnp.where(gz > 0, -1, 8192))
+        row = row + place(0.6 * upper[2] * v[7], here, jnp.where(gz < AXES[2] - 1, 4, 8192))
+        for j in range(4):
+            own = w[2 * j] + w[2 * j + 1] - 0.6 * (totals[2 * j] * v[2 * j] + totals[2 * j + 1] * v[2 * j + 1])
+            to_next = v[2 * j] + v[2 * j - 1] if j > 0 else v[2 * j]
+            to_last = v[2 * j + 1] + v[2 * j + 2] if j < 3 else v[2 * j + 1]
+            row = row + place(own + 0.6 * (upper[2] * to_next + lower[2] * to_last), here, j)
+        for d, up, down in ((0, offset(1, 0), offset(-1, 0)), (1, offset(0, 1), offset(0, -1))):
+            for j in range(4):
+                row = row + place(upper[d] * pair[j], up, j) + place(lower[d] * pair[j], down, j)
+        return jnp.sum(row, axis=0, keepdims=True) * (1.0 / 128.0)
+
+    def correct(picked, source, iterate, left, totals, at):
         tiles = [jnp.broadcast_to(picked[8 * t : 8 * t + 8], (8, 128)) for t in range(78)]
         own, x_up, x_down, y_up, y_down = tiles[:6], tiles[6:10], tiles[10:14], tiles[14:18], tiles[18:22]
         rest, scaled = [], []
@@ -550,45 +569,55 @@
     def scale(a, b):
         return [p * q for p, q in zip(a, b)]
 
-    def remainder(source, iterate, at):
-        own_part = local_part(iterate)
+    def remainder(source, own_part, iterate, at):
         wait_halo(at)
         return minus(source, minus(own_part, couple(iterate, ghosts(at))))
 
-    first = [0.6 * a for a in scale(right, inverse)]
+    totals, shifts = prepare()
+    spread = scale(right, inverse)
+    first = [0.6 * a for a in spread]
+    columns = [(shifts[2 * j] + shifts[2 * j + 1])[:, :1] for j in range(4)]
+    message = [cell_row(columns, 0.125), cell_message(right, spread, totals)]
+    own_part = local_part(first)
     pl.semaphore_wait(barrier, DEVICES - 1)
     send_halo(0, first)
-    totals, shifts = prepare()
-    columns = [(shifts[2 * j] + shifts[2 * j + 1])[:, :1] for j in range(4)]
-    tell(0, cell_row(columns, 0.125))
-    left = remainder(right, first, 0)
-    tell(1, cell_sums(left))
+    tell(0, jnp.concatenate(message, axis=1))
+    left = remainder(right, own_part, first, 0)
     send_halo(1, scale(left, inverse), inverse, scale(totals, inverse))
-    coarse = coarse_matrix(hear(0), beside_ref[...])
-    cells_ref[...] = exact_dot(pick_ref[...], coarse)
-    z0, w0 = correct(hear(1), right, first, left, totals, 1)
-
-    start = [0.6 * a for a in scale(w0, inverse)]
+    heard = hear(0)
+    shift_row = [jnp.sum(heard[:16, :, :128], axis=0), jnp.sum(heard[16:, :, :128], axis=0)]
+    cells = jnp.sum(heard[:, :, 128:], axis=0)
+    coarse = coarse_matrix(jnp.concatenate(shift_row, axis=1), beside_ref[...])
+    coarse_ref[...] = coarse
+    column = jnp.sum(coarse * cells, axis=1, keepdims=True)
+    same = iota((CELLS, CELLS), 0) == iota((CELLS, CELLS), 1)
+    row = jnp.sum(jnp.where(same, column, 0.0), axis=0, keepdims=True)
+    picked = jnp.sum(pick_ref[...].astype(f32) * row, axis=1, keepdims=True)
+    z0, w0 = correct(picked, right, first, left, totals, 1)
+
+    spread = scale(w0, inverse)
+    start = [0.6 * a for a in spread]
     send_halo(2, start)
-    early_dots = dots((right, z0), (z0, w0))
-    left = remainder(w0, start, 2)
-    tell(2, jnp.concatenate([cell_sums(left), early_dots], axis=1))
+    message = [cell_message(w0, spread, totals), dots((right, z0), (z0, w0))]
+    tell(1, jnp.concatenate(message, axis=1))
+    own_part = local_part(start)
+    left = remainder(w0, own_part, start, 2)
     send_halo(3, scale(left, inverse))
-    heard = hear(2)
-    heard_dots = jnp.sum(note_in[2, :, :, 128:], axis=0)
-    gamma, curve = heard_dots[:, 0:1], heard_dots[:, 1:2]
+    cells_ref[...] = exact_dot(pick_ref[...], coarse_ref[...], 3)
+    heard = jnp.sum(hear(1), axis=0)
+    gamma, curve = heard[:, CELLS : CELLS + 1], heard[:, CELLS + 1 : CELLS + 2]
     alpha = gamma / curve
-    u, v = correct(heard, w0, start, left, totals, 3)
+    picked = jnp.sum(cells_ref[...] * heard[:, :CELLS], axis=1, keepdims=True)
+    u, v = correct(picked, w0, start, left, totals, 3)
     z1 = [a - alpha * b for a, b in zip(z0, u)]
     w1 = [a - alpha * b for a, b in zip(w0, v)]
     r1 = [a - alpha * b for a, b in zip(right, w0)]
-    tell(3, dots((r1, z1), (z1, w1), (z1, w0), (z0, w1)))
+    tell(2, dots((r1, z1), (z1, w1), (z1, w0), (z0, w1)))
     for at in range(HALO_ROUNDS):
         end_halo(at)
-    for at in range(3):
+    for at in range(2):
         end_tell(at)
-    heard = hear(3)
-    heard = heard[:, :128] + heard[:, 128:]
+    heard = jnp.sum(hear(2), axis=0)
     gamma_2 = heard[:, 0:1]
     beta = gamma_2 / gamma
     curve_2 = heard[:, 1:2] + beta * (heard[:, 2:3] + heard[:, 3:4]) + beta * beta * curve
@@ -598,7 +627,7 @@
     whole = jnp.concatenate(halves(field) + halves(rest), axis=1)
     for x in range(4):
         out_ref[x] = whole[2 * x : 2 * x + 2, :]
-    end_tell(3)
+    end_tell(2)
 
 
 def per_device_fused(right_side, element_class, class_blocks, class_shift, face_weights):
@@ -617,17 +646,18 @@
             pltpu.SMEM(face_weights.shape, f32),
             pltpu.VMEM((HALO_ROUNDS, 24, 8, 128), f32),
             pltpu.VMEM((HALO_ROUNDS, 24, 8, 128), f32),
-            pltpu.VMEM((HALO_ROUNDS, 1, MESSAGE), f32),
-            pltpu.VMEM((HALO_ROUNDS, DEVICES, 1, MESSAGE), f32),
+            pltpu.VMEM((NOTE_ROUNDS, 1, MESSAGE), f32),
+            pltpu.VMEM((NOTE_ROUNDS, DEVICES, 1, MESSAGE), f32),
             pltpu.VMEM((1024, 128), jnp.bfloat16),
             pltpu.VMEM((624, CELLS), f32),
+            pltpu.VMEM((CELLS, CELLS), f32),
             pltpu.VMEM((624, CELLS), jnp.bfloat16),
             pltpu.VMEM((CELLS, CELLS), jnp.bfloat16),
             pltpu.SemaphoreType.DMA((5,)),
             pltpu.SemaphoreType.DMA((HALO_ROUNDS, 6)),
             pltpu.SemaphoreType.DMA((HALO_ROUNDS, 6)),
-            pltpu.SemaphoreType.DMA((HALO_ROUNDS,)),
-            pltpu.SemaphoreType.DMA((HALO_ROUNDS,)),
+            pltpu.SemaphoreType.DMA((NOTE_ROUNDS,)),
+            pltpu.SemaphoreType.DMA((NOTE_ROUNDS,)),
         ],
         compiler_params=pltpu.CompilerParams(
             collective_id=0, has_side_effects=True

time: 30.1 us -> 27.6 us (0.917)
  Pallas kernels: 27.9 us -> 25.4 us
    pallas_call x1, Pallas kernels: 27.9 us -> 25.4 us  [per_device_fused(): pl.pallas_call(fused, out_shape=jax.ShapeDtypeStruct((size_x, size_y, 2 *...]
where the time goes in v6:
time: 27.6 us; the launch traced here: 27.4 us
  Pallas kernels  25.4 us (92%)
  local copies, waits for them, and re-layouts  1.35 us (5%)
  between operations  0.64 us (2%)
    pallas_call x1, Pallas kernels, per_device_fused(): pl.pallas_call(fused, out_shape=jax.ShapeDtypeStruct((size_x, size_y, 2 *...  25.4 us
    slice x1, local copies, waits for them, and re-layouts, per_device_fused(): return (both[:, :, :width], both[:, :, width:])  1.35 us

profile of v6, /device:TPU:0, one launch (start us, length us, event | category | flops | bytes accessed | tf_op | source)
XLA Modules:
  0.0 27.4 jit_solution(3814105866487199429)
XLA Ops:
  0.6 25.4 %shard_map.68 = f32[4,2,1024]{2,1,0:T(2,128)} custom-call(f32[4,2,512]{2,1,0:T(2,128)} %r_hbm.1, s32[4,2,8]{2,1,0:T(2,128)} %class_hbm.1, f32[16,64,64]{2,1,0:T(8,128)} %blocks_hbm.1, f32[16]{0:T(128)} %shift_hbm.1, f32[3]{0:T(128)} %weight_hbm.1), custom_call_target="tpu_custom_call" | custom-call | tf_op jit(solution)/shard_map/pallas_call | solution.py:636
  26.0 1.3 %fusion = (f32[4,2,512]{2,1,0:T(2,128)}, f32[4,2,512]{2,1,0:T(2,128)}) fusion(f32[4,2,1024]{2,1,0:T(2,128)} %shard_map.68), kind=kLoop, calls=%fused_computation | loop fusion | bytes 65536 | tf_op jit(solution)/shard_map/slice | solution.py:666

commit v7 on v6

--- a/solution.py
+++ b/solution.py
@@ -238,19 +238,33 @@
     return jnp.where((apart == 1) & same, 1.0, 0.0).astype(f32)
 
 
-def coarse_matrix(shift_row, beside_1):
-    i, j = iota((CELLS, CELLS), 0), iota((CELLS, CELLS), 1)
-    eye = jnp.where(i == j, 1.0, 0.0).astype(f32)
+def where_one(hit):
+    return jnp.where(hit, 1.0, 0.0).astype(f32)
+
+
+def coarse_constants():
+    beside_1 = neighbours(CELLS, 2, 4, 1, 3)
     beside_2 = neighbours(32, 1, 3, 1, 3)
     j2, cell = iota((32, CELLS), 0), iota((32, CELLS), 1)
-    parent = (cell >> 7) * 16 + (cell >> 5 & 1) * 8 + (cell >> 1 & 7)
-    down_1 = jnp.where(parent == j2, 1.0, 0.0).astype(f32)
+    down_1 = where_one((cell >> 7) * 16 + (cell >> 5 & 1) * 8 + (cell >> 1 & 7) == j2)
     ci, cj = iota((CELLS, 32), 0), iota((CELLS, 32), 1)
-    up_1 = jnp.where((ci >> 7) * 16 + (ci >> 5 & 1) * 8 + (ci >> 1 & 7) == cj, 1.0, 0.0).astype(f32)
+    up_1 = where_one((ci >> 7) * 16 + (ci >> 5 & 1) * 8 + (ci >> 1 & 7) == cj)
     j3, k3 = iota((8, 32), 0), iota((8, 32), 1)
-    down_2 = jnp.where((k3 >> 1 & 3) == j3, 1.0, 0.0).astype(f32)
+    down_2 = where_one((k3 >> 1 & 3) == j3)
     k2, i2 = iota((32, 8), 0), iota((32, 8), 1)
-    up_2 = jnp.where((k2 >> 1 & 3) == i2, 1.0, 0.0).astype(f32)
+    up_2 = where_one((k2 >> 1 & 3) == i2)
+    return (
+        beside_1, beside_2, down_1, exact_dot(down_1, beside_1, 1),
+        jnp.concatenate([up_1, exact_dot(beside_1, up_1, 1)], axis=0),
+        jnp.concatenate([down_2, exact_dot(down_2, beside_2, 1)], axis=1),
+        jnp.concatenate([up_2, exact_dot(beside_2, up_2, 1)], axis=0),
+    )
+
+
+def coarse_matrix(shift_row, constants):
+    beside_1, beside_2, down_1, down_beside_1, up_1, down_2, up_2 = constants
+    i, j = iota((CELLS, CELLS), 0), iota((CELLS, CELLS), 1)
+    eye = where_one(i == j)
     d1_row = 6.0 + shift_row
     d1 = jnp.sum(eye * d1_row, axis=1, keepdims=True)
     d2 = 6.0 + 0.125 * jnp.sum(down_1 * shift_row, axis=1, keepdims=True)
@@ -258,19 +272,22 @@
     d3 = 6.0 + 0.015625 * jnp.sum(
         jnp.where((cellw >> 2 & 3) == j3w, shift_row, 0.0), axis=1, keepdims=True
     )
-    q2 = 0.25 * exact_dot(down_1, 0.4 * eye + 0.6 * beside_1.astype(f32) / d1_row)
+    q2 = 0.1 * down_1 + 0.15 * down_beside_1 / d1_row
     x2 = 0.6 * q2 / d2
-    q3 = 0.25 * exact_dot(down_2, 0.4 * q2 + exact_dot(beside_2, x2))
+    q3 = 0.25 * exact_dot(down_2, jnp.concatenate([0.4 * q2, x2], axis=0))
+    beside_x2 = exact_dot(beside_2, x2)
     x3 = 0.6 * q3 / d3
     row = iota((8, CELLS), 0)
     for _ in range(SWEEPS - 1):
         after = jnp.where(row < 3, pltpu.roll(x3, 7, 0), 0.0)
         before = jnp.where((row > 0) & (row < 4), pltpu.roll(x3, 1, 0), 0.0)
         x3 = 0.4 * x3 + 0.6 * (q3 + after + before) / d3
-    x2 = x2 + exact_dot(up_2, x3)
-    x2 = 0.4 * x2 + 0.6 * (q2 + exact_dot(beside_2, x2)) / d2
-    x1 = 0.6 * eye / d1 + exact_dot(up_1, x2)
-    return 0.4 * x1 + 0.6 * (eye + exact_dot(beside_1, x1)) / d1
+    fine = exact_dot(up_2, x3)
+    x2 = 0.4 * (x2 + fine[:32]) + 0.6 * (q2 + beside_x2 + fine[32:]) / d2
+    fine = exact_dot(up_1, x2)
+    x1 = 0.6 * eye / d1 + fine[:CELLS]
+    beside_x1 = 0.6 * beside_1 / d1_row + fine[CELLS:]
+    return 0.4 * x1 + 0.6 * (eye + beside_x1) / d1
 
 
 def pick_cells(gx, gy, gz):
@@ -298,8 +315,8 @@
 def fused(
     r_hbm, class_hbm, blocks_hbm, shift_hbm, weight_hbm, out_ref,
     r_ref, class_ref, blocks_ref, shift_ref, weight_ref,
-    halo_out, halo_in, note_out, note_in, w_ref, cells_ref, coarse_ref, pick_ref, beside_ref,
-    load_sem, halo_send, halo_recv, note_send, note_recv,
+    halo_out, halo_in, note_out, note_in, w_ref, cells_ref, coarse_ref, pick_ref,
+    load_sem, halo_send, halo_recv, note_send, note_recv, *const_refs,
 ):
     loads = (
         (blocks_hbm, blocks_ref), (r_hbm, r_ref), (class_hbm, class_ref),
@@ -319,7 +336,8 @@
     for to in others:
         pl.semaphore_signal(barrier, inc=1, device_id=to, device_id_type=MESH)
     pick_ref[...] = pick_cells(gx, gy, gz).astype(jnp.bfloat16)
-    beside_ref[...] = neighbours(CELLS, 2, 4, 1, 3).astype(jnp.bfloat16)
+    for ref, value in zip(const_refs, coarse_constants()):
+        ref[...] = value
 
     for load in loads:
         load.wait()
@@ -363,15 +381,15 @@
     diagonal = by_class(diag_rows)
     inverse = [1.0 / d for d in diagonal]
 
-    def prepare():
-        rows = []
+    totals = by_class([twice(jnp.sum(blocks_ref[k], axis=0, keepdims=True)) for k in range(16)])
+    shifts = by_class([shift_ref[k] for k in range(16)])
+
+    def split_blocks():
         for k in range(16):
             rest = jnp.where(eye, 0.0, blocks_ref[k])
             rest_hi = rest.astype(jnp.bfloat16).astype(f32)
             both = jnp.concatenate([rest_hi, rest - rest_hi], axis=1)
             w_ref[64 * k : 64 * k + 64, :] = both.astype(jnp.bfloat16)
-            rows.append(twice(jnp.sum(rest, axis=0, keepdims=True)) + diag_rows[k])
-        return by_class(rows), by_class([shift_ref[k] for k in range(16)])
 
     own_cell = (sub >> 2) * 64 + gy * 16 + gz * 4
 
@@ -573,25 +591,25 @@
         wait_halo(at)
         return minus(source, minus(own_part, couple(iterate, ghosts(at))))
 
-    totals, shifts = prepare()
     spread = scale(right, inverse)
     first = [0.6 * a for a in spread]
     columns = [(shifts[2 * j] + shifts[2 * j + 1])[:, :1] for j in range(4)]
     message = [cell_row(columns, 0.125), cell_message(right, spread, totals)]
-    own_part = local_part(first)
     pl.semaphore_wait(barrier, DEVICES - 1)
     send_halo(0, first)
     tell(0, jnp.concatenate(message, axis=1))
+    split_blocks()
+    own_part = local_part(first)
     left = remainder(right, own_part, first, 0)
     send_halo(1, scale(left, inverse), inverse, scale(totals, inverse))
     heard = hear(0)
     shift_row = [jnp.sum(heard[:16, :, :128], axis=0), jnp.sum(heard[16:, :, :128], axis=0)]
     cells = jnp.sum(heard[:, :, 128:], axis=0)
-    coarse = coarse_matrix(jnp.concatenate(shift_row, axis=1), beside_ref[...])
+    same = iota((CELLS, CELLS), 0) == iota((CELLS, CELLS), 1)
+    column = jnp.sum(jnp.where(same, cells, 0.0), axis=1, keepdims=True)
+    coarse = coarse_matrix(jnp.concatenate(shift_row, axis=1), [ref[...] for ref in const_refs])
     coarse_ref[...] = coarse
-    column = jnp.sum(coarse * cells, axis=1, keepdims=True)
-    same = iota((CELLS, CELLS), 0) == iota((CELLS, CELLS), 1)
-    row = jnp.sum(jnp.where(same, column, 0.0), axis=0, keepdims=True)
+    row = jnp.sum(coarse * column, axis=0, keepdims=True)
     picked = jnp.sum(pick_ref[...].astype(f32) * row, axis=1, keepdims=True)
     z0, w0 = correct(picked, right, first, left, totals, 1)
 
@@ -652,12 +670,18 @@
             pltpu.VMEM((624, CELLS), f32),
             pltpu.VMEM((CELLS, CELLS), f32),
             pltpu.VMEM((624, CELLS), jnp.bfloat16),
-            pltpu.VMEM((CELLS, CELLS), jnp.bfloat16),
             pltpu.SemaphoreType.DMA((5,)),
             pltpu.SemaphoreType.DMA((HALO_ROUNDS, 6)),
             pltpu.SemaphoreType.DMA((HALO_ROUNDS, 6)),
             pltpu.SemaphoreType.DMA((NOTE_ROUNDS,)),
             pltpu.SemaphoreType.DMA((NOTE_ROUNDS,)),
+            pltpu.VMEM((CELLS, CELLS), f32),
+            pltpu.VMEM((32, 32), f32),
+            pltpu.VMEM((32, CELLS), f32),
+            pltpu.VMEM((32, CELLS), f32),
+            pltpu.VMEM((2 * CELLS, 32), f32),
+            pltpu.VMEM((8, 64), f32),
+            pltpu.VMEM((64, 8), f32),
         ],
         compiler_params=pltpu.CompilerParams(
             collective_id=0, has_side_effects=True

time: 27.6 us -> 27 us (0.978)
  Pallas kernels: 25.4 us -> 24.8 us
    pallas_call x1, Pallas kernels: 25.4 us -> 24.8 us  [per_device_fused(): pl.pallas_call(fused, out_shape=jax.ShapeDtypeStruct((size_x, size_y, 2 *...]
where the time goes in v7:
time: 27 us; the launch traced here: 26.8 us
  Pallas kernels  24.8 us (92%)
  local copies, waits for them, and re-layouts  1.35 us (5%)
  between operations  0.64 us (2%)
    pallas_call x1, Pallas kernels, per_device_fused(): pl.pallas_call(fused, out_shape=jax.ShapeDtypeStruct((size_x, size_y, 2 *...  24.8 us
    slice x1, local copies, waits for them, and re-layouts, per_device_fused(): return (both[:, :, :width], both[:, :, width:])  1.35 us

profile of v7, /device:TPU:0, one launch (start us, length us, event | category | flops | bytes accessed | tf_op | source)
XLA Modules:
  0.0 26.8 jit_solution(1789251398642290409)
XLA Ops:
  0.6 24.8 %shard_map.68 = f32[4,2,1024]{2,1,0:T(2,128)} custom-call(f32[4,2,512]{2,1,0:T(2,128)} %r_hbm.1, s32[4,2,8]{2,1,0:T(2,128)} %class_hbm.1, f32[16,64,64]{2,1,0:T(8,128)} %blocks_hbm.1, f32[16]{0:T(128)} %shift_hbm.1, f32[3]{0:T(128)} %weight_hbm.1), custom_call_target="tpu_custom_call" | custom-call | tf_op jit(solution)/shard_map/pallas_call | solution.py:654
  25.4 1.3 %fusion = (f32[4,2,512]{2,1,0:T(2,128)}, f32[4,2,512]{2,1,0:T(2,128)}) fusion(f32[4,2,1024]{2,1,0:T(2,128)} %shard_map.68), kind=kLoop, calls=%fused_computation | loop fusion | bytes 65536 | tf_op jit(solution)/shard_map/slice | solution.py:690

commit v8 on v7

--- a/solution.py
+++ b/solution.py
@@ -318,23 +318,25 @@
     halo_out, halo_in, note_out, note_in, w_ref, cells_ref, coarse_ref, pick_ref,
     load_sem, halo_send, halo_recv, note_send, note_recv, *const_refs,
 ):
-    loads = (
-        (blocks_hbm, blocks_ref), (r_hbm, r_ref), (class_hbm, class_ref),
-        (shift_hbm, shift_ref), (weight_hbm, weight_ref),
-    )
-    loads = [pltpu.make_async_copy(a, b, load_sem.at[i]) for i, (a, b) in enumerate(loads)]
-    for load in loads:
-        load.start()
     gx, gy, gz = lax.axis_index("gx"), lax.axis_index("gy"), lax.axis_index("gz")
 
     me = gx * 16 + gy * 4 + gz
-    ring_y = [gy] + [lax.rem(gy + k, 4) for k in range(1, 4)]
-    ring_z = [gz] + [lax.rem(gz + k, 4) for k in range(1, 4)]
-    others = [(x, y, z) for y in ring_y for x in (gx, 1 - gx) for z in ring_z][:0:-1]
+    flip, chip, core = gy // 2, gz // 2, gz % 2
+    near = gy + flip * (3 - 2 * gy)
+    far_y = [k + flip * (3 - 2 * k) for k in (3, 2, 1 - near)] + [gy]
+    far_z = [2 * (1 - chip) + 1 - core, 2 * (1 - chip) + core, 2 * chip + 1 - core, gz]
+    others = [(x, y, z) for y in far_y for x in (1 - gx, gx) for z in far_z][:-1]
     barrier = pltpu.get_barrier_semaphore()
     halo_in[...] = jnp.zeros_like(halo_in)
     for to in others:
         pl.semaphore_signal(barrier, inc=1, device_id=to, device_id_type=MESH)
+    loads = (
+        (blocks_hbm, blocks_ref), (r_hbm, r_ref), (class_hbm, class_ref),
+        (shift_hbm, shift_ref), (weight_hbm, weight_ref),
+    )
+    loads = [pltpu.make_async_copy(a, b, load_sem.at[i]) for i, (a, b) in enumerate(loads)]
+    for load in loads:
+        load.start()
     pick_ref[...] = pick_cells(gx, gy, gz).astype(jnp.bfloat16)
     for ref, value in zip(const_refs, coarse_constants()):
         ref[...] = value

time: 27 us -> 26.8 us (level)
  no operation moved by 1% of the time
where the time goes in v8:
time: 26.8 us; the launch traced here: 26.6 us
  Pallas kernels  24.6 us (92%)
  local copies, waits for them, and re-layouts  1.35 us (5%)
  between operations  0.64 us (2%)
    pallas_call x1, Pallas kernels, per_device_fused(): pl.pallas_call(fused, out_shape=jax.ShapeDtypeStruct((size_x, size_y, 2 *...  24.6 us
    slice x1, local copies, waits for them, and re-layouts, per_device_fused(): return (both[:, :, :width], both[:, :, width:])  1.35 us

profile of v8, /device:TPU:0, one launch (start us, length us, event | category | flops | bytes accessed | tf_op | source)
XLA Modules:
  0.0 26.6 jit_solution(12362713720684236433)
XLA Ops:
  0.6 24.6 %shard_map.68 = f32[4,2,1024]{2,1,0:T(2,128)} custom-call(f32[4,2,512]{2,1,0:T(2,128)} %r_hbm.1, s32[4,2,8]{2,1,0:T(2,128)} %class_hbm.1, f32[16,64,64]{2,1,0:T(8,128)} %blocks_hbm.1, f32[16]{0:T(128)} %shift_hbm.1, f32[3]{0:T(128)} %weight_hbm.1), custom_call_target="tpu_custom_call" | custom-call | tf_op jit(solution)/shard_map/pallas_call | solution.py:656
  25.2 1.3 %fusion = (f32[4,2,512]{2,1,0:T(2,128)}, f32[4,2,512]{2,1,0:T(2,128)}) fusion(f32[4,2,1024]{2,1,0:T(2,128)} %shard_map.68), kind=kLoop, calls=%fused_computation | loop fusion | bytes 65536 | tf_op jit(solution)/shard_map/slice | solution.py:692

commit v9 on v8

--- a/solution.py
+++ b/solution.py
@@ -338,8 +338,6 @@
     for load in loads:
         load.start()
     pick_ref[...] = pick_cells(gx, gy, gz).astype(jnp.bfloat16)
-    for ref, value in zip(const_refs, coarse_constants()):
-        ref[...] = value
 
     for load in loads:
         load.wait()
@@ -602,6 +600,8 @@
     tell(0, jnp.concatenate(message, axis=1))
     split_blocks()
     own_part = local_part(first)
+    for ref, value in zip(const_refs, coarse_constants()):
+        ref[...] = value
     left = remainder(right, own_part, first, 0)
     send_halo(1, scale(left, inverse), inverse, scale(totals, inverse))
     heard = hear(0)
@@ -632,7 +632,7 @@
     z1 = [a - alpha * b for a, b in zip(z0, u)]
     w1 = [a - alpha * b for a, b in zip(w0, v)]
     r1 = [a - alpha * b for a, b in zip(right, w0)]
-    tell(2, dots((r1, z1), (z1, w1), (z1, w0), (z0, w1)))
+    tell(2, dots((r1, z1), (z1, w1), (z1, w0)))
     for at in range(HALO_ROUNDS):
         end_halo(at)
     for at in range(2):
@@ -640,7 +640,7 @@
     heard = jnp.sum(hear(2), axis=0)
     gamma_2 = heard[:, 0:1]
     beta = gamma_2 / gamma
-    curve_2 = heard[:, 1:2] + beta * (heard[:, 2:3] + heard[:, 3:4]) + beta * beta * curve
+    curve_2 = heard[:, 1:2] + beta * (2.0 * heard[:, 2:3] + beta * curve)
     alpha_2 = gamma_2 / curve_2
     field = [alpha * a + alpha_2 * (b + beta * a) for a, b in zip(z0, z1)]
     rest = [a - alpha_2 * (b + beta * c) for a, b, c in zip(r1, w1, w0)]

time: 26.8 us -> 26.8 us (level)
  no operation moved by 1% of the time
where the time goes in v9:
time: 26.8 us; the launch traced here: 26.6 us
  Pallas kernels  24.6 us (92%)
  local copies, waits for them, and re-layouts  1.35 us (5%)
  between operations  0.64 us (2%)
    pallas_call x1, Pallas kernels, per_device_fused(): pl.pallas_call(fused, out_shape=jax.ShapeDtypeStruct((size_x, size_y, 2 *...  24.6 us
    slice x1, local copies, waits for them, and re-layouts, per_device_fused(): return (both[:, :, :width], both[:, :, width:])  1.35 us

profile of v9, /device:TPU:0, one launch (start us, length us, event | category | flops | bytes accessed | tf_op | source)
XLA Modules:
  0.0 26.6 jit_solution(1315117913632690938)
XLA Ops:
  0.6 24.6 %shard_map.68 = f32[4,2,1024]{2,1,0:T(2,128)} custom-call(f32[4,2,512]{2,1,0:T(2,128)} %r_hbm.1, s32[4,2,8]{2,1,0:T(2,128)} %class_hbm.1, f32[16,64,64]{2,1,0:T(8,128)} %blocks_hbm.1, f32[16]{0:T(128)} %shift_hbm.1, f32[3]{0:T(128)} %weight_hbm.1), custom_call_target="tpu_custom_call" | custom-call | tf_op jit(solution)/shard_map/pallas_call | solution.py:656
  25.2 1.3 %fusion = (f32[4,2,512]{2,1,0:T(2,128)}, f32[4,2,512]{2,1,0:T(2,128)}) fusion(f32[4,2,1024]{2,1,0:T(2,128)} %shard_map.68), kind=kLoop, calls=%fused_computation | loop fusion | bytes 65536 | tf_op jit(solution)/shard_map/slice | solution.py:692
